TPU v7x, 256 devices: a whole 4x4x8 slice. The times are simulated.
256 devices in a mesh: section: 8 (over z), blk: 32 (over y, x, core).
Axes of the slice: x: 4, y: 4, z: 8, core: 2. Of those that a mesh axis runs over, the one named last changes fastest.
Arguments:
- raw: bfloat16 [8, 4096, 8192], P('section', 'blk'), may hold values from -6 to 6
- pair_blocks: int32 [32, 2], replicated, may hold values from 0 to 31
Outputs:
- stacked: float32 [32, 128, 1024], P('blk', 'section')
All inputs are finite; a program needn't handle non-finite values.
Results may differ from a plain program's by a relative error of at most 0.0029.
Values may be sent and summed in bfloat16 or wider, within the bound.
No kernel may reach another device: no remote copies, remote signals or barrier semaphores. Data moves between devices by JAX's collectives and lax.ppermute only.
A program may use at most 128 MiB of HBM per device.

v0:
```python
import math

import jax
import jax.numpy as jnp
from jax import lax
from jax.sharding import PartitionSpec as P

CB = 128
LAGS = 1024
PB_DEV = 1


def phase_table(first, second, modulus):
    phase = first[:, None] * second[None, :] % modulus
    angle = phase.astype(jnp.float32) * jnp.float32(2.0 * math.pi / modulus)
    return (jnp.cos(angle), jnp.sin(angle))


def spectrum(trace):
    rows, length = trace.shape
    outer = length // 128
    high = lax.Precision.HIGHEST
    signal = trace.astype(jnp.float32)
    signal = signal - jnp.mean(signal, axis=-1, keepdims=True)
    signal = signal.reshape(rows, 128, outer).transpose(0, 2, 1)
    inner_idx = jnp.arange(128, dtype=jnp.int32)
    outer_idx = jnp.arange(outer, dtype=jnp.int32)
    cos_inner, sin_inner = phase_table(inner_idx, inner_idx, 128)
    first_real = jnp.einsum("rnm,mk->rnk", signal, cos_inner, precision=high)
    first_imag = -jnp.einsum("rnm,mk->rnk", signal, sin_inner, precision=high)
    cos_twist, sin_twist = phase_table(outer_idx, inner_idx, length)
    twist_real = first_real * cos_twist + first_imag * sin_twist
    twist_imag = first_imag * cos_twist - first_real * sin_twist
    cos_outer, sin_outer = phase_table(outer_idx, outer_idx, outer)
    spec_real = jnp.einsum("rnk,nm->rmk", twist_real, cos_outer, precision=high)
    spec_real = spec_real + jnp.einsum("rnk,nm->rmk", twist_imag, sin_outer, precision=high)
    spec_imag = jnp.einsum("rnk,nm->rmk", twist_imag, cos_outer, precision=high)
    spec_imag = spec_imag - jnp.einsum("rnk,nm->rmk", twist_real, sin_outer, precision=high)
    return (spec_real.reshape(rows, length), spec_imag.reshape(rows, length))


def whiten(trace):
    real_part, imag_part = spectrum(trace)
    power = real_part * real_part + imag_part * imag_part
    level = jnp.mean(power, axis=-1, keepdims=True)
    scale = lax.rsqrt(power + 0.1 * level + 1e-06)
    return ((real_part * scale).astype(jnp.bfloat16), (imag_part * scale).astype(jnp.bfloat16))


def lag_rows(first_bin, count, length):
    bins = first_bin + jnp.arange(count, dtype=jnp.int32)
    shifts = (jnp.arange(LAGS, dtype=jnp.int32) - LAGS // 2) % length
    cosine, sine = phase_table(bins, shifts, length)
    return jnp.concatenate([cosine.astype(jnp.bfloat16), -sine.astype(jnp.bfloat16)], axis=0)


def body(raw, pair_blocks):
    seg_count, rows, length = raw.shape
    real_part, imag_part = whiten(raw[0])
    real_list = [real_part]
    imag_list = [imag_part]
    spectra = jnp.stack([jnp.stack(real_list), jnp.stack(imag_list)])
    band_spec = lax.all_to_all(spectra, "blk", split_axis=3, concat_axis=2, tiled=True)
    owners = lax.axis_size("blk")
    band = length // owners
    first_bin = lax.axis_index("blk") * band
    blocks = band_spec.reshape(2, seg_count, -1, CB, band)
    table = lag_rows(first_bin, band, length)
    left = jnp.take(blocks, pair_blocks[:, 0], axis=2).astype(jnp.float32)
    right = jnp.take(blocks, pair_blocks[:, 1], axis=2).astype(jnp.float32)
    cross_real = (left[0] * right[0] + left[1] * right[1]).astype(jnp.bfloat16)
    cross_imag = (left[1] * right[0] - left[0] * right[1]).astype(jnp.bfloat16)
    cross_real, cross_imag = (cross_real, cross_imag)
    joined = jnp.concatenate([cross_real, cross_imag], axis=-1)
    lagged = jnp.einsum("spck,kl->pcl", joined, table, preferred_element_type=jnp.float32)
    summed = lax.psum_scatter(
        lagged.reshape(PB_DEV * CB * lax.axis_size("blk"), LAGS),
        "blk",
        scatter_dimension=0,
        tiled=True,
    )
    result = (summed * jnp.float32(length ** (-0.5))).reshape(PB_DEV, CB, LAGS)
    return lax.psum_scatter(result, "section", scatter_dimension=1, tiled=True)


def solution(mesh):
    in_specs = (P("section", "blk", None), P())
    out_specs = P("blk", "section", None)
    return jax.shard_map(body, mesh=mesh, in_specs=in_specs, out_specs=out_specs, check_vma=False)
```

profile of v0, /device:TPU:2, one launch (start us, length us, event | category | flops | bytes accessed | tf_op | source)
XLA Modules:
  0.0 360.6 jit_solution(17919391136289918899)
XLA Ops:
  6.5 0.1 fusion.55
  6.7 3.2 copy.44
  9.9 1.1 convert_reduce_fusion
  11.0 2.5 subtract_bitcast_fusion.1
  13.6 5.4 %copy.45 = f32[128,64,128]{2,0,1:T(8,128)} copy(f32[128,64,128]{0,1,2:T(8,128)} %subtract_bitcast_fusion.1) | data formatting | bytes 8388608 | tf_op jit(solution)/shard_map/transpose | solution.py:25
  19.0 6.3 %fusion.28 = f32[128,64,128]{2,0,1:T(8,128)S(1)} fusion(f32[128,64,128]{2,0,1:T(8,128)} %copy.45), kind=kOutput, calls=%fused_computation.52 | convolution fusion | flops 1610842112 | bytes 8388608 | tf_op jit(solution)/shard_map/rnm,mk->rnk/dot_general | solution.py:30
  25.3 4.5 %multiply_add_fusion = (f32[128,64,128]{2,0,1:T(8,128)S(1)}, f32[128,64,128]{2,0,1:T(8,128)S(1)}) fusion(f32[128,64,128]{2,0,1:T(8,128)S(1)} %fusion.28, f32[64,128]{1,0:T(8,128)S(1)} %get-tuple-element.20, f32[64,128]{1,0:T(8,128)S(1)} %get-tuple-element.21, f32[128,64,128]{2,0,1:T(8,128)S(1)} %copy-done.1), kind=kOutput, calls=%fused_computation.20 | convolution fusion | flops 1618182144 | bytes 16842752 | tf_op jit(solution)/shard_map/rnm,mk->rnk/dot_general | solution.py:29
  29.8 6.3 %fusion.8 = f32[64,128,128]{2,0,1:T(8,128)S(1)} fusion(f32[128,64,128]{2,0,1:T(8,128)S(1)} %get-tuple-element.13), kind=kOutput, calls=%fused_computation.24 | convolution fusion | flops 805363712 | bytes 8388608 | tf_op jit(solution)/shard_map/rnk,nm->rmk/dot_general | solution.py:36
  36.1 9.6 %fusion.6 = f32[64,128,128]{2,0,1:T(8,128)} fusion(f32[128,64,128]{2,0,1:T(8,128)S(1)} %get-tuple-element.13), kind=kOutput, calls=%fused_computation.22 | convolution fusion | flops 805363712 | bytes 8388608 | tf_op jit(solution)/shard_map/rnk,nm->rmk/dot_general | solution.py:37
  45.7 9.1 %add_bitcast_fusion = f32[128,64,128]{2,1,0:T(8,128)} fusion(f32[64,128,128]{2,0,1:T(8,128)S(1)} %fusion.8, f32[128,64,128]{2,0,1:T(8,128)S(1)} %get-tuple-element.12), kind=kOutput, calls=%fused_computation.18 | convolution fusion | flops 806412288 | bytes 12582912 | tf_op jit(solution)/shard_map/rnk,nm->rmk/dot_general | solution.py:35
  54.8 5.1 %reshape.269 = f32[1,1,128,8192]{3,2,1,0:T(8,128)} reshape(f32[128,64,128]{2,1,0:T(8,128)} %add_bitcast_fusion) | data formatting | bytes 8388608 | tf_op jit(solution)/shard_map/reshape | solution.py:39
  59.9 13.0 %add_reduce_fusion = (f32[128]{0:T(128)S(1)}, f32[128,64,128]{2,1,0:T(8,128)}) fusion(f32[128,64,128]{2,1,0:T(8,128)} %add_bitcast_fusion, f32[64,128,128]{2,0,1:T(8,128)} %fusion.6, f32[128,64,128]{2,0,1:T(8,128)} %copy-done), kind=kOutput, calls=%fused_computation.16 | convolution fusion | flops 810606464 | bytes 16777728 | tf_op jit(solution)/shard_map/rnk,nm->rmk/dot_general | solution.py:38
  72.9 5.0 %reshape.270 = f32[1,1,128,8192]{3,2,1,0:T(8,128)} reshape(f32[128,64,128]{2,1,0:T(8,128)} %get-tuple-element.19) | data formatting | bytes 8388608 | tf_op jit(solution)/shard_map/reshape | solution.py:39
  77.9 4.8 %multiply_convert_fusion.1 = (bf16[1,1,128,8192]{3,2,1,0:T(8,128)(2,1)S(1)}, bf16[1,1,128,8192]{3,2,1,0:T(8,128)(2,1)S(1)}) fusion(f32[1,1,128,8192]{3,2,1,0:T(8,128)} %reshape.269, f32[1,1,128,8192]{3,2,1,0:T(8,128)} %reshape.270, f32[128]{0:T(128)S(1)} %broadcast_multiply_fusion), kind=kLoop, calls=%fused_computation.14 | loop fusion | flops 9437184 | bytes 12583424 | tf_op jit(solution)/shard_map/convert_element_type | solution.py:47
  82.7 2.3 pad_maximum_fusion
  85.1 11.1 %copy.51 = bf16[2,1,128,8192]{2,0,1,3:T(2,128)(2,1)} copy(bf16[2,1,128,8192]{3,2,1,0:T(8,128)(2,1)} %pad_maximum_fusion) | data formatting | bytes 8388608 | tf_op jit(solution)/shard_map/stack | solution.py:62
  96.2 7.8 %all-to-all-start = ((bf16[2,1,128,8192]{2,0,1,3:T(2,128)(2,1)}), bf16[2,1,128,8192]{2,0,1,3:T(2,128)(2,1)}, u32[]{:S(2)}, u32[]{:S(2)}) async-start(bf16[2,1,128,8192]{2,0,1,3:T(2,128)(2,1)} %copy.51), calls=%async_computation | async-start | bytes 8388608 | tf_op jit(solution)/shard_map/all_to_all | solution.py:63
  104.2 4.4 %cosine_convert_fusion = bf16[256,1024]{1,0:T(8,128)(2,1)S(1)} fusion(s32[1024]{0:T(1024)S(1)} %add_select_fusion.4, s32[256]{0:T(256)S(1)} %iota_add_fusion), kind=kLoop, calls=%fused_computation.43 | loop fusion | flops 3932160 | bytes 529408 | tf_op jit(solution)/shard_map/convert_element_type | solution.py:54
  108.5 4.2 %fusion.24 = bf16[256,1024]{1,0:T(8,128)(2,1)S(1)} fusion(s32[1024]{0:T(1024)S(1)} %add_select_fusion.4, s32[256]{0:T(256)S(1)} %iota_add_fusion), kind=kLoop, calls=%fused_computation.44 | loop fusion | flops 4718592 | bytes 529408 | tf_op jit(solution)/shard_map/neg | solution.py:54
  112.8 42.6 %all-to-all-done = bf16[2,1,128,8192]{2,0,1,3:T(2,128)(2,1)} async-done(((bf16[2,1,128,8192]{2,0,1,3:T(2,128)(2,1)}), bf16[2,1,128,8192]{2,0,1,3:T(2,128)(2,1)}, u32[]{:S(2)}, u32[]{:S(2)}) %all-to-all-start) | async-done | bytes 4194336 | tf_op jit(solution)/shard_map/all_to_all | solution.py:63
  155.4 11.1 %copy.53 = bf16[2,1,128,32,256]{4,2,3,0,1:T(8,128)(2,1)} copy(bf16[2,1,128,32,256]{2,0,4,3,1:T(2,128)(2,1)} %bitcast.9) | data formatting | bytes 8388608 | tf_op jit(solution)/shard_map/all_to_all | solution.py:63
  166.5 5.0 %gather_fusion = bf16[32,2,128,256]{3,2,1,0:T(8,128)(2,1)} fusion(bf16[2,32,128,256]{3,2,1,0:T(8,128)(2,1)} %bitcast.57, s32[1024]{0:T(1024)S(1)} %get-tuple-element.23), kind=kCustom, calls=%fused_computation.clone | custom fusion | bytes 8388736 | tf_op jit(solution)/shard_map/jit(_take)/gather | solution.py:69
  171.5 5.0 %gather_fusion.1 = bf16[32,2,128,256]{3,2,1,0:T(8,128)(2,1)} fusion(bf16[2,32,128,256]{3,2,1,0:T(8,128)(2,1)} %bitcast.58, s32[1024]{0:T(1024)S(1)} %get-tuple-element.22), kind=kCustom, calls=%fused_computation.1.clone | custom fusion | bytes 8388736 | tf_op jit(solution)/shard_map/jit(_take)/gather | solution.py:70
  176.5 2.9 fusion.5
  179.4 0.5 copy-done.2
  179.9 0.6 fusion.4
  180.6 2.2 add_convert_fusion
  182.8 8.1 %fusion = f32[4096,1024]{1,0:T(8,128)} fusion(bf16[4096,256]{1,0:T(8,128)(2,1)S(1)} %bitcast.61, bf16[4096,256]{1,0:T(8,128)(2,1)S(1)} %bitcast.60, bf16[256,1024]{1,0:T(8,128)(2,1)S(1)} %fusion.24, bf16[256,1024]{1,0:T(8,128)(2,1)S(1)} %cosine_convert_fusion), kind=kOutput, calls=%fused_computation.3 | convolution fusion | flops 4305453056 | bytes 22020096 | tf_op jit(solution)/shard_map/spck,kl->pcl/dot_general | solution.py:75
  190.9 0.0 reduce-scatter.5.cloned.1.call-start
  191.0 123.2 %reduce-scatter.3.cloned.1.call-done = f32[128,1024]{1,0:T(8,128)} async-done(((f32[4096,1024]{1,0:T(8,128)}), f32[128,1024]{1,0:T(8,128)}) %reduce-scatter.3.cloned.1.call-update) | async-done | bytes 524304 | tf_op jit(solution)/shard_map/reduce_scatter | solution.py:76
  314.2 1.9 multiply_bitcast_fusion
  316.1 37.4 %reduce-scatter.5.cloned.1.call-done = f32[1,16,1024]{2,1,0:T(8,128)} async-done(((f32[1,128,1024]{2,1,0:T(8,128)}), f32[1,16,1024]{2,1,0:T(8,128)}) %reduce-scatter.5.cloned.1.call-update) | async-done | bytes 65552 | tf_op jit(solution)/shard_map/reduce_scatter | solution.py:83
  (16 shorter events, 0.1 us)
Async XLA Ops:
  19.0 6.3 %copy-start.1 = (f32[128,64,128]{2,0,1:T(8,128)S(1)}, f32[128,64,128]{2,0,1:T(8,128)}, u32[]{:S(2)}) copy-start(f32[128,64,128]{2,0,1:T(8,128)} %copy.45) | copy-start | bytes 12582916
  29.8 15.9 %copy-start = (f32[128,64,128]{2,0,1:T(8,128)}, f32[128,64,128]{2,0,1:T(8,128)S(1)}, u32[]{:S(2)}) copy-start(f32[128,64,128]{2,0,1:T(8,128)S(1)} %get-tuple-element.12) | copy-start | bytes 12582916
  96.2 7.9 %copy-start.3 = (s32[32,2]{0,1:T(2,128)S(1)}, s32[32,2]{0,1:T(2,128)}, u32[]{:S(2)}) copy-start(s32[32,2]{0,1:T(2,128)} %param.5) | copy-start | bytes 772
  96.2 59.2 %all-to-all-start = ((bf16[2,1,128,8192]{2,0,1,3:T(2,128)(2,1)}), bf16[2,1,128,8192]{2,0,1,3:T(2,128)(2,1)}, u32[]{:S(2)}, u32[]{:S(2)}) async-start(bf16[2,1,128,8192]{2,0,1,3:T(2,128)(2,1)} %copy.51), calls=%async_computation | async-start | bytes 8388608 | tf_op jit(solution)/shard_map/all_to_all | solution.py:63
  104.0 210.1 %reduce-scatter.3.cloned.1.call-start = ((), (), s32[]{:S(2)}) async-start(), calls=%async_computation.3 | async-start | bytes 17301504 | tf_op jit(solution)/shard_map/reduce_scatter | solution.py:76
  176.5 3.4 copy-start.2
  190.9 162.6 %reduce-scatter.5.cloned.1.call-start = ((), (), s32[]{:S(2)}) async-start(), calls=%async_computation.4 | async-start | bytes 589824 | tf_op jit(solution)/shard_map/reduce_scatter | solution.py:83
Sparse Core Ops, SparseCore 0:
  191.0 123.0 reduce-scatter.2
  316.7 36.7 reduce-scatter.4
where the time goes:
time: 365 us; the launch traced here: 361 us
  waiting for transfers between devices  203 us (56%)
  matrix products  56.9 us (16%)
  local copies, waits for them, and re-layouts  51.4 us (14%)
  other arithmetic  27.3 us (7%)
  between operations  13.8 us (4%)
  starting transfers between devices  7.89 us (2%)
    reduce_scatter x1, waiting for transfers between devices, body(): lax.psum_scatter(lagged.reshape(PB_DEV * CB * lax.axis_size('blk'), LAGS)...  123 us
    all_to_all x1, waiting for transfers between devices, body(): lax.all_to_all(spectra, 'blk', split_axis=3, concat_axis=2, tiled=True)  42.6 us
    reduce_scatter x1, waiting for transfers between devices, body(): return lax.psum_scatter(result, 'section', scatter_dimension=1, tiled=True)  37.4 us
    dot_general x1, matrix products, spectrum(): jnp.einsum('rnk,nm->rmk', twist_real, sin_outer, precision=high)  13 us
    another operation x1, local copies, waits for them, and re-layouts, body(): spectra = jnp.stack([jnp.stack(real_list), jnp.stack(imag_list)])  11.1 us
    all_to_all x1, local copies, waits for them, and re-layouts, body(): lax.all_to_all(spectra, 'blk', split_axis=3, concat_axis=2, tiled=True)  11.1 us
    reshape x2, local copies, waits for them, and re-layouts, spectrum(): return (spec_real.reshape(rows, length), spec_imag.reshape(rows, length))  10.1 us
    dot_general x1, matrix products, spectrum(): spec_imag = jnp.einsum('rnk,nm->rmk', twist_imag, cos_outer, precision=high)  9.57 us
  transfers between devices with their start and end apart: 3, of which 3 were waited for; matrix products, arithmetic and copies ran while one was open for 2% of the time, Pallas kernels for 0%

commit v1 on v0

v1 whole, which is shorter than its diff:
```python
import math

import jax
import jax.numpy as jnp
import ml_dtypes
import numpy as np
from jax import lax
from jax.experimental import pallas as pl
from jax.experimental.pallas import tpu as pltpu
from jax.sharding import PartitionSpec as P

NF = 8192
LAGS = 1024
LANES = 128
ROWS = 16
SLOTS = 32
HALF = math.sqrt(0.5)
AXES = ("section", "blk")
RESIDUES = (
    [8, 16, 24]
    + [4 + 8 * r for r in range(4)]
    + [q + 8 * r for q in (1, 2, 3) for r in range(8)]
)


def bin_numbers():
    lane = np.arange(LANES)
    first = np.where(lane < 64, 64 * (lane + 1), 32 + 64 * (lane - 64))
    return np.stack([first] + [r + 64 * lane for r in RESIDUES])


def twiddles():
    lane = np.arange(LANES)
    turns = [lane / 128.0, lane / 256.0 + lane / 2.0] + [lane * r / NF for r in RESIDUES]
    angle = 2.0 * np.pi * np.stack(turns)
    return np.stack([np.cos(angle), np.sin(angle)]).astype(np.float32)


def last_transform():
    index = np.arange(LANES)
    angle = 2.0 * np.pi * (index[:, None] * index[None, :] % LANES) / LANES
    cosine, sine = np.cos(angle), np.sin(angle)
    full = np.block([[cosine, -sine], [sine, cosine]])
    high = full.astype(ml_dtypes.bfloat16)
    low = (full - high.astype(np.float64)).astype(ml_dtypes.bfloat16)
    return np.stack([high, low])


def lag_table():
    bins = bin_numbers()
    shifts = (np.arange(LAGS) - LAGS // 2) % NF
    angle = 2.0 * np.pi * (bins.reshape(-1)[:, None] * shifts[None, :] % NF) / NF
    weight = np.where(bins.reshape(-1) == NF // 2, 0.5, 1.0)[:, None]
    cosine = np.cos(angle).astype(ml_dtypes.bfloat16).astype(np.float32) * weight
    sine = np.sin(angle).astype(ml_dtypes.bfloat16).astype(np.float32) * weight
    return np.concatenate([cosine, -sine]).astype(ml_dtypes.bfloat16)


def real8(x):
    s0, d0, s2, d2 = x[0] + x[4], x[0] - x[4], x[2] + x[6], x[2] - x[6]
    s1, d1, s3, d3 = x[1] + x[5], x[1] - x[5], x[3] + x[7], x[3] - x[7]
    even, odd = s0 + s2, s1 + s3
    u, v = (d1 - d3) * HALF, (d1 + d3) * HALF
    return [
        (even + odd, None),
        (d0 + u, -(d2 + v)),
        (s0 - s2, s3 - s1),
        (d0 - u, d2 - v),
        (even - odd, None),
    ]


def complex8(re, im):
    def add(i, j):
        return (i[0] + j[0], i[1] + j[1])

    def sub(i, j):
        return (i[0] - j[0], i[1] - j[1])

    def sub_i(i, j):
        return (i[0] + j[1], i[1] - j[0])

    def add_i(i, j):
        return (i[0] - j[1], i[1] + j[0])

    t = list(zip(re, im))
    a0, a1, a2, a3 = add(t[0], t[4]), sub(t[0], t[4]), add(t[2], t[6]), sub(t[2], t[6])
    a4, a5, a6, a7 = add(t[1], t[5]), sub(t[1], t[5]), add(t[3], t[7]), sub(t[3], t[7])
    b0, b2, b1, b3 = add(a0, a2), sub(a0, a2), sub_i(a1, a3), add_i(a1, a3)
    b4, b6, b5, b7 = add(a4, a6), sub(a4, a6), sub_i(a5, a7), add_i(a5, a7)
    c5 = ((b5[0] + b5[1]) * HALF, (b5[1] - b5[0]) * HALF)
    c7 = ((b7[1] - b7[0]) * HALF, (b7[0] + b7[1]) * -HALF)
    return [
        add(b0, b4), add(b1, c5), sub_i(b2, b6), add(b3, c7),
        sub(b0, b4), sub(b1, c5), add_i(b2, b6), sub(b3, c7),
    ]


def whiten_kernel(raw_ref, twist_ref, last_ref, out_ref, part_ref, high_ref, low_ref, spec_ref, turn_ref):
    f32, bf16 = jnp.float32, jnp.bfloat16

    def put(slot, re, im):
        cosine, sine = twist_ref[0, slot : slot + 1, :], twist_ref[1, slot : slot + 1, :]
        if im is None:
            zr, zi = re * cosine, re * -sine
        else:
            zr, zi = re * cosine + im * sine, im * cosine - re * sine
        rows = pl.ds(slot * ROWS, ROWS)
        for z, lanes in ((zr, pl.ds(0, LANES)), (zi, pl.ds(LANES, LANES))):
            high = z.astype(bf16)
            high_ref[rows, lanes] = high
            low_ref[rows, lanes] = (z - high.astype(f32)).astype(bf16)

    for b in range(8):
        x = [raw_ref[0, :, pl.ds((8 * a + b) * LANES, LANES)].astype(f32) for a in range(8)]
        y = real8(x)
        for q in range(5):
            part_ref[0, q, b] = y[q][0]
            if y[q][1] is not None:
                part_ref[1, q, b] = y[q][1]
    whole = real8([part_ref[0, 0, b] for b in range(8)])
    zero = whole[0][0] - jnp.mean(whole[0][0], axis=-1, keepdims=True)
    put(0, zero, None)
    put(1, whole[4][0], None)
    for r in (1, 2, 3):
        put(1 + r, *whole[r])
    slot = 5
    for q in (4, 1, 2, 3):
        re, im = [], []
        for b in range(8):
            cosine, sine = math.cos(2 * math.pi * b * q / 64), math.sin(2 * math.pi * b * q / 64)
            yr = part_ref[0, q, b]
            if q == 4:
                re.append(yr * cosine if b else yr)
                im.append(yr * -sine if b else jnp.zeros_like(yr))
            else:
                yi = part_ref[1, q, b]
                re.append(yr * cosine + yi * sine if b else yr)
                im.append(yi * cosine - yr * sine if b else yi)
        z = complex8(re, im)
        for r in range(4 if q == 4 else 8):
            put(slot, *z[r])
            slot += 1

    high, low = high_ref[...], low_ref[...]
    spec = jnp.dot(high, last_ref[0], preferred_element_type=f32)
    spec = spec + jnp.dot(high, last_ref[1], preferred_element_type=f32)
    spec = spec + jnp.dot(low, last_ref[0], preferred_element_type=f32)
    spec_ref[...] = spec

    lane = lax.broadcasted_iota(jnp.int32, (ROWS, LANES), 1)

    def get(slot):
        re = spec_ref[pl.ds((slot + 1) * ROWS, ROWS), pl.ds(0, LANES)]
        im = spec_ref[pl.ds((slot + 1) * ROWS, ROWS), pl.ds(LANES, LANES)]
        if slot == 0:
            re = jnp.where(lane < 64, spec_ref[pl.ds(0, ROWS), pl.ds(0, LANES)], re)
            im = jnp.where(lane < 64, spec_ref[pl.ds(0, ROWS), pl.ds(LANES, LANES)], im)
        return re, im

    total = None
    for slot in range(SLOTS):
        re, im = get(slot)
        power = re * re + im * im
        if slot == 0:
            power = jnp.where(lane == 63, power * 0.5, power)
        total = power if total is None else total + power
    level = jnp.sum(total, axis=-1, keepdims=True) * (2.0 / NF)
    floor = jnp.broadcast_to(0.1 * level + 1e-06, (ROWS, LANES))
    for slot in range(SLOTS):
        re, im = get(slot)
        scale = lax.rsqrt(re * re + im * im + floor)
        turn_ref[pl.ds(slot, ROWS, stride=2 * SLOTS), :] = re * scale
        turn_ref[pl.ds(slot + SLOTS, ROWS, stride=2 * SLOTS), :] = im * scale
    out_ref[0, :, 0, 0] = turn_ref[...].astype(bf16).reshape(ROWS, 2 * SLOTS, LANES)


def whiten(raw):
    steps = raw.shape[1] // ROWS
    return pl.pallas_call(
        whiten_kernel,
        grid=(steps,),
        out_shape=jax.ShapeDtypeStruct((2, ROWS, 2, 2, 2 * SLOTS, LANES), jnp.bfloat16),
        in_specs=[
            pl.BlockSpec((1, ROWS, NF), lambda g: (0, g, 0)),
            pl.BlockSpec((2, SLOTS + 1, LANES), lambda g: (0, 0, 0)),
            pl.BlockSpec((2, 2 * LANES, 2 * LANES), lambda g: (0, 0, 0)),
        ],
        out_specs=pl.BlockSpec(
            (1, ROWS, 1, 1, 2 * SLOTS, LANES), lambda g: (g % 2, 0, g // 4, (g // 2) % 2, 0, 0)
        ),
        scratch_shapes=[
            pltpu.VMEM((2, 5, 8, ROWS, LANES), jnp.float32),
            pltpu.VMEM(((SLOTS + 1) * ROWS, 2 * LANES), jnp.bfloat16),
            pltpu.VMEM(((SLOTS + 1) * ROWS, 2 * LANES), jnp.bfloat16),
            pltpu.VMEM(((SLOTS + 1) * ROWS, 2 * LANES), jnp.float32),
            pltpu.VMEM((ROWS * 2 * SLOTS, LANES), jnp.float32),
        ],
        compiler_params=pltpu.CompilerParams(vmem_limit_bytes=32 * 2**20),
        name="whiten",
    )(raw, jnp.asarray(twiddles()), jnp.asarray(last_transform()))


def lag_kernel(pairs_ref, spec_ref, table_ref, keep_ref, send_ref, cross_ref, left_ref, turn_ref):
    f32, bf16 = jnp.float32, jnp.bfloat16

    def one(i, carry):
        first, second = pairs_ref[0, i], pairs_ref[1, i]
        for h in range(2):
            for j in range(2):
                a = spec_ref[h * 32 + first, j].astype(f32)
                b = spec_ref[h * 32 + second, j].astype(f32)
                ar, ai, br, bi = a[:SLOTS], a[SLOTS:], b[:SLOTS], b[SLOTS:]
                row = pl.multiple_of(((h * 2 + j) * 32 + i) * 2 * SLOTS, 2 * SLOTS)
                cross_ref[pl.ds(row, SLOTS), :] = ar * br + ai * bi
                cross_ref[pl.ds(row + SLOTS, SLOTS), :] = ai * br - ar * bi
        return carry

    lax.fori_loop(0, 32, one, 0)
    for slot in range(2 * SLOTS):
        left_ref[:, pl.ds(slot * LANES, LANES)] = cross_ref[pl.ds(slot, 128, stride=2 * SLOTS), :].astype(bf16)
    lags = jnp.dot(left_ref[...], table_ref[...], preferred_element_type=f32)
    lags = (lags[:64] + lags[64:]) * (2.0 * NF**-0.5)
    for q in range(8):
        turn_ref[pl.ds(q, 64, stride=8), :] = lags[:, q * LANES : (q + 1) * LANES]
    turned = turn_ref[...].reshape(2, 2, 16, 8, LANES)
    keep_ref[...] = turned[:, 0].astype(bf16)
    send_ref[...] = turned[:, 1].astype(bf16)


def correlate(pairs, spectra):
    half = jax.ShapeDtypeStruct((2, 16, 8, LANES), jnp.bfloat16)
    vmem = pl.BlockSpec(memory_space=pltpu.VMEM)
    return pl.pallas_call(
        lag_kernel,
        out_shape=(half, half),
        in_specs=[pl.BlockSpec(memory_space=pltpu.SMEM), vmem, vmem],
        out_specs=(vmem, vmem),
        scratch_shapes=[
            pltpu.VMEM((128 * 2 * SLOTS, LANES), jnp.float32),
            pltpu.VMEM((128, NF), jnp.bfloat16),
            pltpu.VMEM((64 * 8, LANES), jnp.float32),
        ],
        compiler_params=pltpu.CompilerParams(vmem_limit_bytes=48 * 2**20),
        name="correlate",
    )(pairs, spectra, jnp.asarray(lag_table()))


def stack_kernel(lags_ref, out_ref, turn_ref):
    total = lags_ref[0].astype(jnp.float32)
    for t in range(1, 4):
        total = total + lags_ref[t].astype(jnp.float32)
    turn_ref[...] = total.reshape(16 * 8, LANES)
    for q in range(8):
        out_ref[0, :, pl.ds(q * LANES, LANES)] = turn_ref[pl.ds(q, 16, stride=8), :]


def stack(lags):
    vmem = pl.BlockSpec(memory_space=pltpu.VMEM)
    return pl.pallas_call(
        stack_kernel,
        out_shape=jax.ShapeDtypeStruct((1, 16, LAGS), jnp.float32),
        in_specs=[vmem],
        out_specs=vmem,
        scratch_shapes=[pltpu.VMEM((16 * 8, LANES), jnp.float32)],
        name="stack",
    )(lags)


def body(raw, pair_blocks):
    core = lax.axis_index("blk") % 2
    near = [[32 * (2 * t + h) + d for h in range(2) for d in range(32)] for t in range(4)]
    far = [
        [32 * (2 * t + h) + 2 * chip + c for t in range(4) for chip in range(16)]
        for h in range(2)
        for c in range(2)
    ]
    spectra = whiten(raw).reshape(64, 2 * 2 * SLOTS, LANES)
    spectra = lax.all_to_all(spectra, AXES, 0, 0, axis_index_groups=near, tiled=True)
    spectra = spectra.reshape(64, 2, 2 * SLOTS, LANES)
    order = pair_blocks.reshape(16, 2, 2)
    order = jnp.where(core == 0, order, order[:, ::-1]).transpose(2, 1, 0).reshape(2, 32)
    keep, send = correlate(order, spectra)
    got = lax.ppermute(send, "blk", [(i, i ^ 1) for i in range(32)])
    lags = jnp.where(core == 0, jnp.stack([keep, got]), jnp.stack([got, keep]))
    lags = lax.all_to_all(lags.reshape(64, 8, LANES), AXES, 0, 0, axis_index_groups=far, tiled=True)
    return stack(lags.reshape(4, 16, 8, LANES))


def solution(mesh):
    in_specs = (P("section", "blk", None), P())
    out_specs = P("blk", "section", None)
    return jax.shard_map(body, mesh=mesh, in_specs=in_specs, out_specs=out_specs, check_vma=False)
```

time: 365 us -> 91.7 us (0.25)
  waiting for transfers between devices: 203 us -> 28.6 us
  matrix products: 56.9 us -> 0 us
  local copies, waits for them, and re-layouts: 51.4 us -> 4.99 us
  other arithmetic: 27.3 us -> 0.02 us
  blocking collectives: 0 us -> 24.4 us
  Pallas kernels: 0 us -> 22.8 us
  between operations: 13.8 us -> 0.06 us
    reduce_scatter x2 -> x0, waiting for transfers between devices: 161 us -> none  [the longest x1 123 us: body(): lax.psum_scatter(lagged.reshape(PB_DEV * CB * lax.axis_size('blk'), LAGS)...]
    dot_general x7 -> x0, matrix products: 56.9 us -> none  [the longest x1 13 us: spectrum(): jnp.einsum('rnk,nm->rmk', twist_real, sin_outer, precision=high)]
    all_to_all x0 -> x1, blocking collectives: none -> 24.4 us  [body(): lax.all_to_all(lags.reshape(64, 8, LANES), AXES, 0, 0, axis_index_groups=...]
    pallas_call x0 -> x3, Pallas kernels: none -> 22.8 us  [the longest x1 11.1 us: correlate(): pl.pallas_call(lag_kernel, out_shape=(half, half), in_specs=[pl.BlockSpec...]
    all_to_all x1, waiting for transfers between devices: 42.6 us -> 27.5 us  [body(): lax.all_to_all(spectra, AXES, 0, 0, axis_index_groups=near, tiled=True)]
    convert_element_type x5 -> x0, other arithmetic: 15 us -> none  [the longest x1 4.85 us: whiten(): (real_part * scale).astype(jnp.bfloat16)]
    another operation x1 -> x0, local copies, waits for them, and re-layouts: 11.1 us -> none  [body(): spectra = jnp.stack([jnp.stack(real_list), jnp.stack(imag_list)])]
    all_to_all x1 -> x0, local copies, waits for them, and re-layouts: 11.1 us -> none  [body(): lax.all_to_all(spectra, 'blk', split_axis=3, concat_axis=2, tiled=True)]
  transfers between devices with their start and end apart: 3 -> 2, of which waited for: 3 -> 2; matrix products, arithmetic and copies ran while one was open for 2% -> 0% of each run, Pallas kernels for 0% -> 0%
where the time goes in v1:
time: 91.7 us; the launch traced here: 90.7 us
  waiting for transfers between devices  28.6 us (31%)
  blocking collectives  24.4 us (27%)
  Pallas kernels  22.8 us (25%)
  starting transfers between devices  9.72 us (11%)
  local copies, waits for them, and re-layouts  4.99 us (5%)
    all_to_all x1, waiting for transfers between devices, body(): lax.all_to_all(spectra, AXES, 0, 0, axis_index_groups=near, tiled=True)  27.5 us
    all_to_all x1, blocking collectives, body(): lax.all_to_all(lags.reshape(64, 8, LANES), AXES, 0, 0, axis_index_groups=...  24.4 us
    pallas_call x1, Pallas kernels, correlate(): pl.pallas_call(lag_kernel, out_shape=(half, half), in_specs=[pl.BlockSpec...  11.1 us
    pallas_call x1, Pallas kernels, whiten(): pl.pallas_call(whiten_kernel, grid=(steps,), out_shape=jax.ShapeDtypeStru...  10.2 us
    all_to_all x1, starting transfers between devices, body(): lax.all_to_all(spectra, AXES, 0, 0, axis_index_groups=near, tiled=True)  9.51 us
    unnamed x10, local copies, waits for them, and re-layouts  4.66 us
  transfers between devices with their start and end apart: 2, of which 2 were waited for; matrix products, arithmetic and copies ran while one was open for 0% of the time, Pallas kernels for 0%

profile of v1, /device:TPU:2, one launch (start us, length us, event | category | flops | bytes accessed | tf_op | source)
XLA Modules:
  0.0 90.7 jit_solution(15304853220049225359)
XLA Ops:
  0.0 0.0 copy-start.1
  0.0 1.6 %copy-done.1 = bf16[1,128,8192]{2,1,0:T(8,128)(2,1)S(1)} copy-done((bf16[1,128,8192]{2,1,0:T(8,128)(2,1)S(1)}, bf16[1,128,8192]{2,1,0:T(8,128)(2,1)}, u32[]{:S(2)}) %copy-start.1) | copy-done | bytes 2097176
  1.6 0.0 copy-start.2
  1.6 0.9 %copy-done.2 = bf16[2,256,256]{2,1,0:T(8,128)(2,1)S(1)} copy-done((bf16[2,256,256]{2,1,0:T(8,128)(2,1)S(1)}, bf16[2,256,256]{2,1,0:T(8,128)(2,1)}, u32[]{:S(2)}) %copy-start.2) | copy-done | bytes 262168
  2.5 0.0 copy-start.3
  2.5 0.8 copy-done.3
  3.3 10.2 %whiten.1 = bf16[2,16,2,2,64,128]{5,4,3,2,1,0:T(8,128)(2,1)S(1)} custom-call(bf16[1,128,8192]{2,1,0:T(8,128)(2,1)S(1)} %copy-done.1, f32[2,33,128]{2,1,0:T(8,128)S(1)} %copy-done.3, bf16[2,256,256]{2,1,0:T(8,128)(2,1)S(1)} %copy-done.2), custom_call_target="tpu_custom_call" | custom-call | tf_op jit(solution)/shard_map/whiten/pallas_call | solution.py:180
  13.5 0.0 copy-start
  13.5 1.3 %copy-done = bf16[2,16,2,2,64,128]{5,4,3,2,1,0:T(8,128)(2,1)} copy-done((bf16[2,16,2,2,64,128]{5,4,3,2,1,0:T(8,128)(2,1)}, bf16[2,16,2,2,64,128]{5,4,3,2,1,0:T(8,128)(2,1)S(1)}, u32[]{:S(2)}) %copy-start) | copy-done | bytes 2097176
  14.8 0.0 copy-start.4
  14.8 9.5 %all-to-all-start = ((bf16[64,128,128]{2,1,0:T(8,128)(2,1)}), bf16[64,128,128]{2,1,0:T(8,128)(2,1)S(1)}, u32[]{:S(2)}, u32[]{:S(2)}) async-start(bf16[64,128,128]{2,1,0:T(8,128)(2,1)} %bitcast.11), calls=%async_computation | async-start | bytes 4194304 | tf_op jit(solution)/shard_map/all_to_all | solution.py:279
  24.4 0.0 copy-done.4
  24.4 0.1 reshape.20
  24.5 0.1 rev.3
  24.5 0.1 copy.7
  24.6 0.1 reshape.21.pairs_ref
  24.7 27.5 %all-to-all-done = bf16[64,128,128]{2,1,0:T(8,128)(2,1)S(1)} async-done(((bf16[64,128,128]{2,1,0:T(8,128)(2,1)}), bf16[64,128,128]{2,1,0:T(8,128)(2,1)S(1)}, u32[]{:S(2)}, u32[]{:S(2)}) %all-to-all-start) | async-done | bytes 2097184 | tf_op jit(solution)/shard_map/all_to_all | solution.py:279
  52.2 11.1 %correlate.1 = (bf16[2,16,8,128]{3,2,1,0:T(8,128)(2,1)S(1)}, bf16[2,16,8,128]{3,2,1,0:T(8,128)(2,1)S(1)}) custom-call(s32[2,32]{1,0:T(2,128)S(1)} %reshape.21.pairs_ref, bf16[64,2,64,128]{3,2,1,0:T(8,128)(2,1)S(1)} %bitcast.10, bf16[8192,1024]{1,0:T(8,128)(2,1)} %constant.26.clone.table_ref), custom_call_target="tpu_custom_call" | custom-call | tf_op jit(solution)/shard_map/correlate/pallas_call | solution.py:234
  63.3 0.2 collective-permute-start
  63.5 1.1 %collective-permute-done = bf16[2,16,8,128]{3,2,1,0:T(8,128)(2,1)S(1)} collective-permute-done((bf16[2,16,8,128]{3,2,1,0:T(8,128)(2,1)S(1)}, bf16[2,16,8,128]{3,2,1,0:T(8,128)(2,1)S(1)}, u32[]{:S(2)}, u32[]{:S(2)}) %collective-permute-start) | collective-permute-done | bytes 65568 | tf_op jit(solution)/shard_map/ppermute | solution.py:284
  64.6 24.4 %all_to_all.10 = bf16[64,8,128]{2,1,0:T(8,128)(2,1)} all-to-all(bf16[64,8,128]{2,1,0:T(8,128)(2,1)S(1)} %bitcast.13), channel_id=1, replica_groups={{0,2,4,6,8,10,12,14,16,18,20,22,24,26,28,30,64,66,68,70,72,74,76,78,80,..., dimensions={0} | all-to-all | bytes 262144 | tf_op jit(solution)/shard_map/all_to_all | solution.py:286
  89.1 1.6 %stack.19 = f32[1,16,1024]{2,1,0:T(8,128)} custom-call(bf16[4,16,8,128]{3,2,1,0:T(8,128)(2,1)} %bitcast.14), custom_call_target="tpu_custom_call" | custom-call | tf_op jit(solution)/shard_map/stack/pallas_call | solution.py:260
  (2 shorter events, 0.0 us)
Async XLA Ops:
  0.0 1.6 %copy-start.1 = (bf16[1,128,8192]{2,1,0:T(8,128)(2,1)S(1)}, bf16[1,128,8192]{2,1,0:T(8,128)(2,1)}, u32[]{:S(2)}) copy-start(bf16[1,128,8192]{2,1,0:T(8,128)(2,1)} %raw_ref.1) | copy-start | bytes 6291460
  1.6 0.9 %copy-start.2 = (bf16[2,256,256]{2,1,0:T(8,128)(2,1)S(1)}, bf16[2,256,256]{2,1,0:T(8,128)(2,1)}, u32[]{:S(2)}) copy-start(bf16[2,256,256]{2,1,0:T(8,128)(2,1)} %constant.25.clone.last_ref) | copy-start | bytes 786436
  2.5 0.8 copy-start.3
  13.5 1.3 %copy-start = (bf16[2,16,2,2,64,128]{5,4,3,2,1,0:T(8,128)(2,1)}, bf16[2,16,2,2,64,128]{5,4,3,2,1,0:T(8,128)(2,1)S(1)}, u32[]{:S(2)}) copy-start(bf16[2,16,2,2,64,128]{5,4,3,2,1,0:T(8,128)(2,1)S(1)} %whiten.1) | copy-start | bytes 6291460
  14.8 9.5 %copy-start.4 = (s32[32,2]{0,1:T(2,128)S(1)}, s32[32,2]{0,1:T(2,128)}, u32[]{:S(2)}) copy-start(s32[32,2]{0,1:T(2,128)} %param.6) | copy-start | bytes 772
  14.8 37.4 %all-to-all-start = ((bf16[64,128,128]{2,1,0:T(8,128)(2,1)}), bf16[64,128,128]{2,1,0:T(8,128)(2,1)S(1)}, u32[]{:S(2)}, u32[]{:S(2)}) async-start(bf16[64,128,128]{2,1,0:T(8,128)(2,1)} %bitcast.11), calls=%async_computation | async-start | bytes 4194304 | tf_op jit(solution)/shard_map/all_to_all | solution.py:279
  63.3 1.3 %collective-permute-start = (bf16[2,16,8,128]{3,2,1,0:T(8,128)(2,1)S(1)}, bf16[2,16,8,128]{3,2,1,0:T(8,128)(2,1)S(1)}, u32[]{:S(2)}, u32[]{:S(2)}) collective-permute-start(bf16[2,16,8,128]{3,2,1,0:T(8,128)(2,1)S(1)} %get-tuple-element.8), channel_id=1, source_target_pairs={{0,1},{1,0},{2,3},{3,2},{4,5},{5,4},{6,7},{7,6},{8,9},{9,8},{10,11... | collective-permute-start | bytes 196616 | tf_op jit(solution)/shard_map/ppermute | solution.py:284

commit v2 on v1

--- a/solution.py
+++ b/solution.py
@@ -12,8 +12,11 @@
 NF = 8192
 LAGS = 1024
 LANES = 128
-ROWS = 16
+ROWS = 32
+STEPS = 4
 SLOTS = 32
+TURN = 72
+CHUNKS = 4
 HALF = math.sqrt(0.5)
 AXES = ("section", "blk")
 RESIDUES = (
@@ -43,17 +46,22 @@
     full = np.block([[cosine, -sine], [sine, cosine]])
     high = full.astype(ml_dtypes.bfloat16)
     low = (full - high.astype(np.float64)).astype(ml_dtypes.bfloat16)
-    return np.stack([high, low])
-
-
-def lag_table():
-    bins = bin_numbers()
-    shifts = (np.arange(LAGS) - LAGS // 2) % NF
-    angle = 2.0 * np.pi * (bins.reshape(-1)[:, None] * shifts[None, :] % NF) / NF
-    weight = np.where(bins.reshape(-1) == NF // 2, 0.5, 1.0)[:, None]
-    cosine = np.cos(angle).astype(ml_dtypes.bfloat16).astype(np.float32) * weight
-    sine = np.sin(angle).astype(ml_dtypes.bfloat16).astype(np.float32) * weight
-    return np.concatenate([cosine, -sine]).astype(ml_dtypes.bfloat16)
+    return np.concatenate([high, high, low])
+
+
+def lag_tables():
+    bins = bin_numbers().reshape(-1)
+    weight = np.where(bins == NF // 2, 0.5, 1.0)[:, None]
+    angle = 2.0 * np.pi * (bins[:, None] * np.arange(LAGS // 2)[None, :] % NF) / NF
+    cosine, sine = np.cos(angle), np.sin(angle)
+    sine[:, 0] = np.sin(2.0 * np.pi * (bins * (LAGS // 2) % NF) / NF)
+    tables = np.stack([cosine, sine]).astype(ml_dtypes.bfloat16).astype(np.float32) * weight
+    return tables.astype(ml_dtypes.bfloat16).reshape(2 * CHUNKS, -1, LAGS // 2)
+
+
+def far_cosines():
+    bins = bin_numbers()[:, LANES - 1]
+    return [float(c) for c in np.cos(2.0 * np.pi * (bins * 512 % NF) / NF).astype(ml_dtypes.bfloat16)]
 
 
 def real8(x):
@@ -96,7 +104,7 @@
     ]
 
 
-def whiten_kernel(raw_ref, twist_ref, last_ref, out_ref, part_ref, high_ref, low_ref, spec_ref, turn_ref):
+def outer_transform(raw_ref, twist_ref, high_ref, low_ref, part_ref):
     f32, bf16 = jnp.float32, jnp.bfloat16
 
     def put(slot, re, im):
@@ -112,7 +120,7 @@
             low_ref[rows, lanes] = (z - high.astype(f32)).astype(bf16)
 
     for b in range(8):
-        x = [raw_ref[0, :, pl.ds((8 * a + b) * LANES, LANES)].astype(f32) for a in range(8)]
+        x = [raw_ref[:, pl.ds((8 * a + b) * LANES, LANES)].astype(f32) for a in range(8)]
         y = real8(x)
         for q in range(5):
             part_ref[0, q, b] = y[q][0]
@@ -142,12 +150,14 @@
             put(slot, *z[r])
             slot += 1
 
+def inner_transform(last_ref, high_ref, low_ref, spec_ref):
     high, low = high_ref[...], low_ref[...]
-    spec = jnp.dot(high, last_ref[0], preferred_element_type=f32)
-    spec = spec + jnp.dot(high, last_ref[1], preferred_element_type=f32)
-    spec = spec + jnp.dot(low, last_ref[0], preferred_element_type=f32)
-    spec_ref[...] = spec
-
+    left = jnp.concatenate([high, low, high], axis=1)
+    spec_ref[...] = jnp.dot(left, last_ref[...], preferred_element_type=jnp.float32)
+
+
+def level_rows(spec_ref, out_ref, turn_ref):
+    bf16 = jnp.bfloat16
     lane = lax.broadcasted_iota(jnp.int32, (ROWS, LANES), 1)
 
     def get(slot):
@@ -170,39 +180,94 @@
     for slot in range(SLOTS):
         re, im = get(slot)
         scale = lax.rsqrt(re * re + im * im + floor)
-        turn_ref[pl.ds(slot, ROWS, stride=2 * SLOTS), :] = re * scale
-        turn_ref[pl.ds(slot + SLOTS, ROWS, stride=2 * SLOTS), :] = im * scale
-    out_ref[0, :, 0, 0] = turn_ref[...].astype(bf16).reshape(ROWS, 2 * SLOTS, LANES)
+        turn_ref[pl.ds(slot, ROWS, stride=TURN), :] = re * scale
+        turn_ref[pl.ds(slot + SLOTS, ROWS, stride=TURN), :] = im * scale
+    for r in range(ROWS):
+        out_ref[r // 16, r % 16] = turn_ref[pl.ds(r * TURN, 2 * SLOTS), :].astype(bf16)
+
+
+def whiten_kernel(
+    raw_hbm, twist_hbm, last_hbm, out_hbm, raw_ref, twist_ref, last_ref, out_ref, in_sem, table_sem, out_sem, *work
+):
+    def fetch(g):
+        return pltpu.make_async_copy(raw_hbm.at[0, pl.ds(g * ROWS, ROWS)], raw_ref.at[g], in_sem.at[g])
+
+    def leave(g):
+        return pltpu.make_async_copy(out_ref.at[g], out_hbm.at[:, :, g // 2, g % 2], out_sem.at[g])
+
+    twist = pltpu.make_async_copy(twist_hbm, twist_ref, table_sem.at[0])
+    last = pltpu.make_async_copy(last_hbm, last_ref, table_sem.at[1])
+    fetch(0).start()
+    twist.start()
+    last.start()
+    for g in range(1, STEPS):
+        fetch(g).start()
+    part, high, low, spec, turn = work
+
+    def outer(g):
+        outer_transform(raw_ref.at[g], twist_ref, high, low, part)
+
+    twist.wait()
+    fetch(0).wait()
+    outer(0)
+    last.wait()
+
+    def step(g, carry):
+        fetch(g + 1).wait()
+        inner_transform(last_ref, high, low, spec)
+        outer(g + 1)
+        level_rows(spec, out_ref.at[g], turn)
+
+        leave(g).start()
+        return carry
+
+    lax.fori_loop(0, STEPS - 1, step, 0)
+    inner_transform(last_ref, high, low, spec)
+    level_rows(spec, out_ref.at[STEPS - 1], turn)
+    leave(STEPS - 1).start()
+    for g in range(STEPS):
+        leave(g).wait()
 
 
 def whiten(raw):
-    steps = raw.shape[1] // ROWS
+    far = pl.BlockSpec(memory_space=pltpu.HBM)
     return pl.pallas_call(
         whiten_kernel,
-        grid=(steps,),
-        out_shape=jax.ShapeDtypeStruct((2, ROWS, 2, 2, 2 * SLOTS, LANES), jnp.bfloat16),
-        in_specs=[
-            pl.BlockSpec((1, ROWS, NF), lambda g: (0, g, 0)),
-            pl.BlockSpec((2, SLOTS + 1, LANES), lambda g: (0, 0, 0)),
-            pl.BlockSpec((2, 2 * LANES, 2 * LANES), lambda g: (0, 0, 0)),
-        ],
-        out_specs=pl.BlockSpec(
-            (1, ROWS, 1, 1, 2 * SLOTS, LANES), lambda g: (g % 2, 0, g // 4, (g // 2) % 2, 0, 0)
-        ),
+        out_shape=jax.ShapeDtypeStruct((2, 16, 2, 2, 2 * SLOTS, LANES), jnp.bfloat16),
+        in_specs=[far] * 3,
+        out_specs=far,
         scratch_shapes=[
+            pltpu.VMEM((STEPS, ROWS, NF), jnp.bfloat16),
+            pltpu.VMEM((2, SLOTS + 1, LANES), jnp.float32),
+            pltpu.VMEM((6 * LANES, 2 * LANES), jnp.bfloat16),
+            pltpu.VMEM((STEPS, 2, 16, 2 * SLOTS, LANES), jnp.bfloat16),
+            pltpu.SemaphoreType.DMA((STEPS,)),
+            pltpu.SemaphoreType.DMA((2,)),
+            pltpu.SemaphoreType.DMA((STEPS,)),
+        ]
+        + [
             pltpu.VMEM((2, 5, 8, ROWS, LANES), jnp.float32),
             pltpu.VMEM(((SLOTS + 1) * ROWS, 2 * LANES), jnp.bfloat16),
             pltpu.VMEM(((SLOTS + 1) * ROWS, 2 * LANES), jnp.bfloat16),
             pltpu.VMEM(((SLOTS + 1) * ROWS, 2 * LANES), jnp.float32),
-            pltpu.VMEM((ROWS * 2 * SLOTS, LANES), jnp.float32),
+            pltpu.VMEM((ROWS * TURN, LANES), jnp.float32),
         ],
-        compiler_params=pltpu.CompilerParams(vmem_limit_bytes=32 * 2**20),
+        compiler_params=pltpu.CompilerParams(vmem_limit_bytes=60 * 2**20),
         name="whiten",
     )(raw, jnp.asarray(twiddles()), jnp.asarray(last_transform()))
 
 
-def lag_kernel(pairs_ref, spec_ref, table_ref, keep_ref, send_ref, cross_ref, left_ref, turn_ref):
+def lag_kernel(
+    pairs_ref, spec_ref, table_hbm, keep_ref, send_ref, cross_ref, left_ref, table_ref, turn_ref, table_sem
+):
     f32, bf16 = jnp.float32, jnp.bfloat16
+    depth = table_ref.shape[1]
+
+    def fetch(c):
+        return pltpu.make_async_copy(table_hbm.at[c], table_ref.at[c], table_sem.at[c])
+
+    for c in range(2 * CHUNKS):
+        fetch(c).start()
 
     def one(i, carry):
         first, second = pairs_ref[0, i], pairs_ref[1, i]
@@ -211,18 +276,43 @@
                 a = spec_ref[h * 32 + first, j].astype(f32)
                 b = spec_ref[h * 32 + second, j].astype(f32)
                 ar, ai, br, bi = a[:SLOTS], a[SLOTS:], b[:SLOTS], b[SLOTS:]
-                row = pl.multiple_of(((h * 2 + j) * 32 + i) * 2 * SLOTS, 2 * SLOTS)
+                row = pl.multiple_of(((h * 2 + j) * 32 + i) * TURN, 8)
                 cross_ref[pl.ds(row, SLOTS), :] = ar * br + ai * bi
                 cross_ref[pl.ds(row + SLOTS, SLOTS), :] = ai * br - ar * bi
         return carry
 
     lax.fori_loop(0, 32, one, 0)
-    for slot in range(2 * SLOTS):
-        left_ref[:, pl.ds(slot * LANES, LANES)] = cross_ref[pl.ds(slot, 128, stride=2 * SLOTS), :].astype(bf16)
-    lags = jnp.dot(left_ref[...], table_ref[...], preferred_element_type=f32)
-    lags = (lags[:64] + lags[64:]) * (2.0 * NF**-0.5)
-    for q in range(8):
-        turn_ref[pl.ds(q, 64, stride=8), :] = lags[:, q * LANES : (q + 1) * LANES]
+    far = None
+    for slot, cosine in enumerate(far_cosines()):
+        cross = cross_ref[pl.ds(slot, 128, stride=TURN), :].astype(bf16)
+        left_ref[:, pl.ds(slot * LANES, LANES)] = cross
+        term = cross.astype(f32)
+        if slot == 0:
+            lane = lax.broadcasted_iota(jnp.int32, (128, LANES), 1)
+            far = jnp.where(lane == 63, 0.5, cosine) * term
+        elif cosine != 0.0:
+            far = far + term * cosine
+    far = jnp.sum(far[:64] + far[64:], axis=-1, keepdims=True)
+    for slot in range(SLOTS, 2 * SLOTS):
+        left_ref[:, pl.ds(slot * LANES, LANES)] = cross_ref[pl.ds(slot, 128, stride=TURN), :].astype(bf16)
+
+    halves = []
+    for part in range(2):
+        total = None
+        for c in range(part * CHUNKS, (part + 1) * CHUNKS):
+            fetch(c).wait()
+            term = jnp.dot(left_ref[:, pl.ds(c * depth, depth)], table_ref[c], preferred_element_type=f32)
+            total = term if total is None else total + term
+        halves.append(total[:64] + total[64:])
+    even, odd = halves
+    lane = lax.broadcasted_iota(jnp.int32, (64, LANES), 1)
+    for q in range(4):
+        e, o = even[:, q * LANES : (q + 1) * LANES], odd[:, q * LANES : (q + 1) * LANES]
+        minus, plus = e + o, e - o
+        if q == 0:
+            minus, plus = jnp.where(lane == 0, far + o, minus), jnp.where(lane == 0, e, plus)
+        turn_ref[pl.ds(q, 64, stride=8), :] = minus * (2.0 * NF**-0.5)
+        turn_ref[pl.ds(q + 4, 64, stride=8), :] = plus * (2.0 * NF**-0.5)
     turned = turn_ref[...].reshape(2, 2, 16, 8, LANES)
     keep_ref[...] = turned[:, 0].astype(bf16)
     send_ref[...] = turned[:, 1].astype(bf16)
@@ -231,19 +321,22 @@
 def correlate(pairs, spectra):
     half = jax.ShapeDtypeStruct((2, 16, 8, LANES), jnp.bfloat16)
     vmem = pl.BlockSpec(memory_space=pltpu.VMEM)
+    tables = pltpu.with_memory_space_constraint(jnp.asarray(lag_tables()), pltpu.HBM)
     return pl.pallas_call(
         lag_kernel,
         out_shape=(half, half),
-        in_specs=[pl.BlockSpec(memory_space=pltpu.SMEM), vmem, vmem],
+        in_specs=[pl.BlockSpec(memory_space=pltpu.SMEM), vmem, pl.BlockSpec(memory_space=pltpu.HBM)],
         out_specs=(vmem, vmem),
         scratch_shapes=[
-            pltpu.VMEM((128 * 2 * SLOTS, LANES), jnp.float32),
+            pltpu.VMEM((128 * TURN, LANES), jnp.float32),
             pltpu.VMEM((128, NF), jnp.bfloat16),
+            pltpu.VMEM(tables.shape, jnp.bfloat16),
             pltpu.VMEM((64 * 8, LANES), jnp.float32),
+            pltpu.SemaphoreType.DMA((2 * CHUNKS,)),
         ],
-        compiler_params=pltpu.CompilerParams(vmem_limit_bytes=48 * 2**20),
+        compiler_params=pltpu.CompilerParams(vmem_limit_bytes=24 * 2**20),
         name="correlate",
-    )(pairs, spectra, jnp.asarray(lag_table()))
+    )(pairs, spectra, tables)
 
 
 def stack_kernel(lags_ref, out_ref, turn_ref):
@@ -251,8 +344,14 @@
     for t in range(1, 4):
         total = total + lags_ref[t].astype(jnp.float32)
     turn_ref[...] = total.reshape(16 * 8, LANES)
-    for q in range(8):
-        out_ref[0, :, pl.ds(q * LANES, LANES)] = turn_ref[pl.ds(q, 16, stride=8), :]
+    runs = [turn_ref[pl.ds(q, 16, stride=8), :] for q in range(8)]
+    lane = lax.broadcasted_iota(jnp.int32, (16, LANES), 1)
+    back = (LANES - lane) % LANES
+    runs[:4] = [jnp.take_along_axis(run, back, axis=1, mode="promise_in_bounds") for run in runs[:4]]
+    for q in range(4):
+        out_ref[0, :, pl.ds(q * LANES, LANES)] = jnp.where(lane == 0, runs[(4 - q) % 4], runs[3 - q])
+    for q in range(4, 8):
+        out_ref[0, :, pl.ds(q * LANES, LANES)] = runs[q]
 
 
 def stack(lags):

time: 91.7 us -> 77.7 us (0.85)
  Pallas kernels: 22.8 us -> 13.7 us
  local copies, waits for them, and re-layouts: 4.99 us -> 0.33 us
    pallas_call x1, Pallas kernels: 11.1 us -> 4.47 us  [correlate(): pl.pallas_call(lag_kernel, out_shape=(half, half), in_specs=[pl.BlockSpec...]
    unnamed x10 -> x2, local copies, waits for them, and re-layouts: 4.66 us -> 0.01 us
    pallas_call x1, Pallas kernels: 10.2 us -> 7.58 us  [whiten(): pl.pallas_call(whiten_kernel, out_shape=jax.ShapeDtypeStruct((2, 16, 2, 2...]
where the time goes in v2:
time: 77.7 us; the launch traced here: 76.8 us
  waiting for transfers between devices  28.6 us (37%)
  blocking collectives  24.4 us (31%)
  Pallas kernels  13.7 us (18%)
  starting transfers between devices  9.59 us (12%)
    all_to_all x1, waiting for transfers between devices, body(): lax.all_to_all(spectra, AXES, 0, 0, axis_index_groups=near, tiled=True)  27.5 us
    all_to_all x1, blocking collectives, body(): lax.all_to_all(lags.reshape(64, 8, LANES), AXES, 0, 0, axis_index_groups=...  24.4 us
    all_to_all x1, starting transfers between devices, body(): lax.all_to_all(spectra, AXES, 0, 0, axis_index_groups=near, tiled=True)  9.39 us
    pallas_call x1, Pallas kernels, whiten(): pl.pallas_call(whiten_kernel, out_shape=jax.ShapeDtypeStruct((2, 16, 2, 2...  7.58 us
    pallas_call x1, Pallas kernels, correlate(): pl.pallas_call(lag_kernel, out_shape=(half, half), in_specs=[pl.BlockSpec...  4.47 us
    pallas_call x1, Pallas kernels, stack(): pl.pallas_call(stack_kernel, out_shape=jax.ShapeDtypeStruct((1, 16, LAGS)...  1.63 us
  transfers between devices with their start and end apart: 2, of which 2 were waited for; matrix products, arithmetic and copies ran while one was open for 0% of the time, Pallas kernels for 0%

profile of v2, /device:TPU:2, one launch (start us, length us, event | category | flops | bytes accessed | tf_op | source)
XLA Modules:
  0.0 76.8 jit_solution(18384122024585972218)
XLA Ops:
  0.0 7.6 %whiten.1 = bf16[2,16,2,2,64,128]{5,4,3,2,1,0:T(8,128)(2,1)} custom-call(bf16[1,128,8192]{2,1,0:T(8,128)(2,1)} %raw_hbm.1, f32[2,33,128]{2,1,0:T(8,128)} %constant.24.clone.twist_hbm, bf16[768,256]{1,0:T(8,128)(2,1)} %constant.25.clone.last_hbm), custom_call_target="tpu_custom_call" | custom-call | tf_op jit(solution)/shard_map/whiten/pallas_call | solution.py:234
  7.6 0.0 copy-start
  7.6 9.4 %all-to-all-start = ((bf16[64,128,128]{2,1,0:T(8,128)(2,1)}), bf16[64,128,128]{2,1,0:T(8,128)(2,1)S(1)}, u32[]{:S(2)}, u32[]{:S(2)}) async-start(bf16[64,128,128]{2,1,0:T(8,128)(2,1)} %bitcast.12), calls=%async_computation | async-start | bytes 4194304 | tf_op jit(solution)/shard_map/all_to_all | solution.py:378
  17.0 0.0 copy-done
  17.0 0.1 reshape.20
  17.1 0.1 rev.3
  17.2 0.1 copy.7
  17.3 0.1 reshape.21.pairs_ref
  17.4 27.5 %all-to-all-done = bf16[64,128,128]{2,1,0:T(8,128)(2,1)S(1)} async-done(((bf16[64,128,128]{2,1,0:T(8,128)(2,1)}), bf16[64,128,128]{2,1,0:T(8,128)(2,1)S(1)}, u32[]{:S(2)}, u32[]{:S(2)}) %all-to-all-start) | async-done | bytes 2097184 | tf_op jit(solution)/shard_map/all_to_all | solution.py:378
  44.8 4.5 %correlate.1 = (bf16[2,16,8,128]{3,2,1,0:T(8,128)(2,1)S(1)}, bf16[2,16,8,128]{3,2,1,0:T(8,128)(2,1)S(1)}) custom-call(s32[2,32]{1,0:T(2,128)S(1)} %reshape.21.pairs_ref, bf16[64,2,64,128]{3,2,1,0:T(8,128)(2,1)S(1)} %bitcast.10, bf16[8,1024,512]{2,1,0:T(8,128)(2,1)} %constant.26.clone.table_hbm), custom_call_target="tpu_custom_call" | custom-call | tf_op jit(solution)/shard_map/correlate/pallas_call | solution.py:325
  49.3 0.2 collective-permute-start
  49.5 1.1 %collective-permute-done = bf16[2,16,8,128]{3,2,1,0:T(8,128)(2,1)S(1)} collective-permute-done((bf16[2,16,8,128]{3,2,1,0:T(8,128)(2,1)S(1)}, bf16[2,16,8,128]{3,2,1,0:T(8,128)(2,1)S(1)}, u32[]{:S(2)}, u32[]{:S(2)}) %collective-permute-start) | collective-permute-done | bytes 65568 | tf_op jit(solution)/shard_map/ppermute | solution.py:383
  50.7 24.4 %all_to_all.10 = bf16[64,8,128]{2,1,0:T(8,128)(2,1)} all-to-all(bf16[64,8,128]{2,1,0:T(8,128)(2,1)S(1)} %bitcast.13), channel_id=1, replica_groups={{0,2,4,6,8,10,12,14,16,18,20,22,24,26,28,30,64,66,68,70,72,74,76,78,80,..., dimensions={0} | all-to-all | bytes 262144 | tf_op jit(solution)/shard_map/all_to_all | solution.py:385
  75.1 1.6 %stack.19 = f32[1,16,1024]{2,1,0:T(8,128)} custom-call(bf16[4,16,8,128]{3,2,1,0:T(8,128)(2,1)} %bitcast.14), custom_call_target="tpu_custom_call" | custom-call | tf_op jit(solution)/shard_map/stack/pallas_call | solution.py:359
  (2 shorter events, 0.0 us)
Async XLA Ops:
  7.6 9.4 %copy-start = (s32[32,2]{0,1:T(2,128)S(1)}, s32[32,2]{0,1:T(2,128)}, u32[]{:S(2)}) copy-start(s32[32,2]{0,1:T(2,128)} %param.6) | copy-start | bytes 772
  7.6 37.2 %all-to-all-start = ((bf16[64,128,128]{2,1,0:T(8,128)(2,1)}), bf16[64,128,128]{2,1,0:T(8,128)(2,1)S(1)}, u32[]{:S(2)}, u32[]{:S(2)}) async-start(bf16[64,128,128]{2,1,0:T(8,128)(2,1)} %bitcast.12), calls=%async_computation | async-start | bytes 4194304 | tf_op jit(solution)/shard_map/all_to_all | solution.py:378
  49.3 1.3 %collective-permute-start = (bf16[2,16,8,128]{3,2,1,0:T(8,128)(2,1)S(1)}, bf16[2,16,8,128]{3,2,1,0:T(8,128)(2,1)S(1)}, u32[]{:S(2)}, u32[]{:S(2)}) collective-permute-start(bf16[2,16,8,128]{3,2,1,0:T(8,128)(2,1)S(1)} %get-tuple-element.8), channel_id=1, source_target_pairs={{0,1},{1,0},{2,3},{3,2},{4,5},{5,4},{6,7},{7,6},{8,9},{9,8},{10,11... | collective-permute-start | bytes 196616 | tf_op jit(solution)/shard_map/ppermute | solution.py:383

commit v3 on v2

v3 whole, which is shorter than its diff:
```python
import math

import jax
import jax.numpy as jnp
import ml_dtypes
import numpy as np
from jax import lax
from jax.experimental import pallas as pl
from jax.experimental.pallas import tpu as pltpu
from jax.sharding import PartitionSpec as P

NF = 8192
LAGS = 1024
LANES = 128
ROWS = 32
STEPS = 4
SLOTS = 32
TURN = 72
CHUNKS = 4
HALF = math.sqrt(0.5)
AXES = ("section", "blk")
RESIDUES = (
    [8, 16, 24]
    + [4 + 8 * r for r in range(4)]
    + [q + 8 * r for q in (1, 2, 3) for r in range(8)]
)


def bin_numbers():
    lane = np.arange(LANES)
    first = np.where(lane % 64 < 32, 64 * lane, 32 + 64 * (lane - 32))
    first[0] = 2048
    return np.stack([first] + [r + 64 * lane for r in RESIDUES])


def twiddles():
    lane = np.arange(LANES)
    turns = [lane / 256.0 - lane / 4.0] + [lane * r / NF for r in RESIDUES]
    angle = 2.0 * np.pi * np.stack(turns)
    return np.stack([np.cos(angle), np.sin(angle)]).astype(np.float32)


def last_transform():
    index = np.arange(LANES)
    angle = 2.0 * np.pi * (index[:, None] * index[None, :] % LANES) / LANES
    cosine, sine = np.cos(angle), np.sin(angle)
    full = np.block([[cosine, -sine], [sine, cosine]])
    return full.astype(np.float32)


def folded_bins():
    bins = bin_numbers()
    return np.concatenate([bins[:16, :64], bins[16:, :64]], axis=1)


def lag_tables():
    bins = folded_bins().reshape(-1)[:, None]
    even, odd = 2 * np.arange(256)[None, :], 2 * np.arange(256)[None, :] + 1
    sign = np.where(np.arange(LANES) < 64, 1.0, -1.0)[None, :, None]
    tables = []
    for function, first in ((np.cos, 0), (np.sin, 512)):
        near = function(2.0 * np.pi * (bins * np.where(even == 0, first, even) % NF) / NF)
        far = function(2.0 * np.pi * (bins * odd % NF) / NF).reshape(16, LANES, 256) * sign
        tables.append(np.concatenate([near, far.reshape(-1, 256)], axis=1))
    return np.stack(tables).astype(ml_dtypes.bfloat16).reshape(2 * CHUNKS, -1, 512)


def far_cosines():
    bins = folded_bins()[:, [1, LANES - 1]]
    cosines = np.cos(2.0 * np.pi * (bins * 512 % NF) / NF).astype(ml_dtypes.bfloat16)
    return [(float(low), float(high)) for low, high in cosines]


def real8(x):
    s0, d0, s2, d2 = x[0] + x[4], x[0] - x[4], x[2] + x[6], x[2] - x[6]
    s1, d1, s3, d3 = x[1] + x[5], x[1] - x[5], x[3] + x[7], x[3] - x[7]
    even, odd = s0 + s2, s1 + s3
    u, v = (d1 - d3) * HALF, (d1 + d3) * HALF
    return [
        (even + odd, None),
        (d0 + u, -(d2 + v)),
        (s0 - s2, s3 - s1),
        (d0 - u, d2 - v),
        (even - odd, None),
    ]


def complex8(re, im):
    def add(i, j):
        return (i[0] + j[0], i[1] + j[1])

    def sub(i, j):
        return (i[0] - j[0], i[1] - j[1])

    def sub_i(i, j):
        return (i[0] + j[1], i[1] - j[0])

    def add_i(i, j):
        return (i[0] - j[1], i[1] + j[0])

    t = list(zip(re, im))
    a0, a1, a2, a3 = add(t[0], t[4]), sub(t[0], t[4]), add(t[2], t[6]), sub(t[2], t[6])
    a4, a5, a6, a7 = add(t[1], t[5]), sub(t[1], t[5]), add(t[3], t[7]), sub(t[3], t[7])
    b0, b2, b1, b3 = add(a0, a2), sub(a0, a2), sub_i(a1, a3), add_i(a1, a3)
    b4, b6, b5, b7 = add(a4, a6), sub(a4, a6), sub_i(a5, a7), add_i(a5, a7)
    c5 = ((b5[0] + b5[1]) * HALF, (b5[1] - b5[0]) * HALF)
    c7 = ((b7[1] - b7[0]) * HALF, (b7[0] + b7[1]) * -HALF)
    return [
        add(b0, b4), add(b1, c5), sub_i(b2, b6), add(b3, c7),
        sub(b0, b4), sub(b1, c5), add_i(b2, b6), sub(b3, c7),
    ]


def outer_transform(raw_ref, twist_ref, turned_ref, part_ref):
    f32 = jnp.float32

    def put(slot, re, im):
        rows = pl.ds(slot * ROWS, ROWS)
        turned_ref[rows, pl.ds(0, LANES)] = re
        turned_ref[rows, pl.ds(LANES, LANES)] = im

    def turn(slot, re, im):
        cosine, sine = twist_ref[0, slot - 1 : slot, :], twist_ref[1, slot - 1 : slot, :]
        if im is None:
            put(slot, re * cosine, re * -sine)
        else:
            put(slot, re * cosine + im * sine, im * cosine - re * sine)

    for b in range(8):
        x = [raw_ref[:, pl.ds((8 * a + b) * LANES, LANES)].astype(f32) for a in range(8)]
        y = real8(x)
        for q in range(5):
            part_ref[0, q, b] = y[q][0]
            if y[q][1] is not None:
                part_ref[1, q, b] = y[q][1]
    whole = real8([part_ref[0, 0, b] for b in range(8)])
    zero = whole[0][0]
    put(0, zero - jnp.mean(zero, axis=-1, keepdims=True), jnp.zeros_like(zero))
    turn(1, whole[4][0], None)
    for r in (1, 2, 3):
        turn(1 + r, *whole[r])
    slot = 5
    for q in (4, 1, 2, 3):
        re, im = [], []
        for b in range(8):
            cosine, sine = math.cos(2 * math.pi * b * q / 64), math.sin(2 * math.pi * b * q / 64)
            yr = part_ref[0, q, b]
            if q == 4:
                re.append(yr * cosine if b else yr)
                im.append(yr * -sine if b else jnp.zeros_like(yr))
            else:
                yi = part_ref[1, q, b]
                re.append(yr * cosine + yi * sine if b else yr)
                im.append(yi * cosine - yr * sine if b else yi)
        z = complex8(re, im)
        for r in range(4 if q == 4 else 8):
            turn(slot, *z[r])
            slot += 1

def inner_transform(last_ref, turned_ref, spec_ref):
    spec_ref[...] = jnp.dot(
        turned_ref[...], last_ref[...], preferred_element_type=jnp.float32, precision=lax.Precision.HIGH
    )


def level_rows(spec_ref, out_ref, turn_ref):
    bf16 = jnp.bfloat16
    lane = lax.broadcasted_iota(jnp.int32, (ROWS, LANES), 1)

    for lanes in (pl.ds(0, LANES), pl.ds(LANES, LANES)):
        whole, moved = spec_ref[pl.ds(0, ROWS), lanes], spec_ref[pl.ds(ROWS, ROWS), lanes]
        whole = jnp.where(lane == 0, pltpu.roll(whole, 96, 1), whole)
        spec_ref[pl.ds(ROWS, ROWS), lanes] = jnp.where(lane % 64 < 32, whole, moved)

    def get(slot):
        rows = pl.ds((slot + 1) * ROWS, ROWS)
        return spec_ref[rows, pl.ds(0, LANES)], spec_ref[rows, pl.ds(LANES, LANES)]

    total = None
    for slot in range(SLOTS):
        re, im = get(slot)
        power = re * re + im * im
        if slot == 0:
            power = jnp.where(lane == 64, power * 0.5, power)
        total = power if total is None else total + power
    level = jnp.sum(total, axis=-1, keepdims=True) * (2.0 / NF)
    floor = jnp.broadcast_to(0.1 * level + 1e-06, (ROWS, LANES))
    for slot in range(SLOTS):
        re, im = get(slot)
        scale = lax.rsqrt(re * re + im * im + floor)
        turn_ref[pl.ds(slot, ROWS, stride=TURN), :] = re * scale
        turn_ref[pl.ds(slot + SLOTS, ROWS, stride=TURN), :] = im * scale
    for r in range(ROWS):
        out_ref[r // 16, r % 16] = turn_ref[pl.ds(r * TURN, 2 * SLOTS), :].astype(bf16)


def whiten_kernel(
    raw_hbm, twist_hbm, last_hbm, out_hbm, raw_ref, twist_ref, last_ref, out_ref, in_sem, table_sem, out_sem, *work
):
    def fetch(g):
        return pltpu.make_async_copy(raw_hbm.at[0, pl.ds(g * ROWS, ROWS)], raw_ref.at[g], in_sem.at[g])

    def leave(g):
        return pltpu.make_async_copy(out_ref.at[g], out_hbm.at[:, :, g // 2, g % 2], out_sem.at[g])

    twist = pltpu.make_async_copy(twist_hbm, twist_ref, table_sem.at[0])
    last = pltpu.make_async_copy(last_hbm, last_ref, table_sem.at[1])
    fetch(0).start()
    twist.start()
    last.start()
    for g in range(1, STEPS):
        fetch(g).start()
    part, turned, spec, turn = work

    def outer(g):
        outer_transform(raw_ref.at[g], twist_ref, turned, part)

    twist.wait()
    fetch(0).wait()
    outer(0)
    last.wait()

    def step(g, carry):
        fetch(g + 1).wait()
        inner_transform(last_ref, turned, spec)
        outer(g + 1)
        level_rows(spec, out_ref.at[g], turn)

        leave(g).start()
        return carry

    lax.fori_loop(0, STEPS - 1, step, 0)
    inner_transform(last_ref, turned, spec)
    level_rows(spec, out_ref.at[STEPS - 1], turn)
    leave(STEPS - 1).start()
    for g in range(STEPS):
        leave(g).wait()


def whiten(raw):
    far = pl.BlockSpec(memory_space=pltpu.HBM)
    return pl.pallas_call(
        whiten_kernel,
        out_shape=jax.ShapeDtypeStruct((2, 16, 2, 2, 2 * SLOTS, LANES), jnp.bfloat16),
        in_specs=[far] * 3,
        out_specs=far,
        scratch_shapes=[
            pltpu.VMEM((STEPS, ROWS, NF), jnp.bfloat16),
            pltpu.VMEM((2, SLOTS, LANES), jnp.float32),
            pltpu.VMEM((2 * LANES, 2 * LANES), jnp.float32),
            pltpu.VMEM((STEPS, 2, 16, 2 * SLOTS, LANES), jnp.bfloat16),
            pltpu.SemaphoreType.DMA((STEPS,)),
            pltpu.SemaphoreType.DMA((2,)),
            pltpu.SemaphoreType.DMA((STEPS,)),
        ]
        + [
            pltpu.VMEM((2, 5, 8, ROWS, LANES), jnp.float32),
            pltpu.VMEM(((SLOTS + 1) * ROWS, 2 * LANES), jnp.float32),
            pltpu.VMEM(((SLOTS + 1) * ROWS, 2 * LANES), jnp.float32),
            pltpu.VMEM((ROWS * TURN, LANES), jnp.float32),
        ],
        compiler_params=pltpu.CompilerParams(vmem_limit_bytes=60 * 2**20),
        name="whiten",
    )(raw, jnp.asarray(twiddles()), jnp.asarray(last_transform()))


def lag_kernel(
    pairs_ref, spec_ref, table_hbm, keep_ref, send_ref, cross_ref, left_ref, table_ref, turn_ref, table_sem
):
    f32, bf16 = jnp.float32, jnp.bfloat16
    depth = table_ref.shape[1]
    half = SLOTS // 2

    def fetch(c):
        return pltpu.make_async_copy(table_hbm.at[c], table_ref.at[c], table_sem.at[c])

    for c in range(2 * CHUNKS):
        fetch(c).start()

    lower = lax.broadcasted_iota(jnp.int32, (half, LANES), 1) < 64

    def one(i, carry):
        pair = pairs_ref[pl.ds(i, 1), :]
        first, second = pair[0, 0], pair[0, 1]
        for h in range(2):
            for j in range(2):
                a = spec_ref[h * 32 + first, j].astype(f32)
                b = spec_ref[h * 32 + second, j].astype(f32)
                ar, ai, br, bi = a[:SLOTS], a[SLOTS:], b[:SLOTS], b[SLOTS:]
                row = pl.multiple_of(((h * 2 + j) * 32 + i) * TURN, 8)
                for part, cross in ((0, ar * br + ai * bi), (1, ai * br - ar * bi)):
                    near = jnp.where(lower, cross[:half], cross[half:])
                    away = pltpu.roll(jnp.where(lower, cross[half:], cross[:half]), 64, 1)
                    cross_ref[pl.ds(row + part * half, half), :] = near
                    cross_ref[pl.ds(row + (2 + part) * half, half), :] = away
        return carry

    lax.fori_loop(0, 32, one, 0, unroll=8)
    lane = lax.broadcasted_iota(jnp.int32, (128, LANES), 1)
    cosines = far_cosines()
    far, middle = None, None
    for side in range(2):
        for slot in range(SLOTS):
            cross = cross_ref[pl.ds(side * SLOTS + slot, 128, stride=TURN), :].astype(bf16)
            term = cross.astype(f32) if slot < half else None
            if side == 1 and slot % half == 0:
                if slot == 0:
                    middle = 0.5 * term[:, :1]
                    term = jnp.where(lane == 0, 0.0, term)
                cross = jnp.where(lane == 0, jnp.zeros_like(cross), cross)
            left_ref[pl.ds(side * 128, 128), pl.ds(slot * LANES, LANES)] = cross
            if slot < half:
                term = term * jnp.where(lane < 64, *cosines[slot])
                far = term if far is None else far + term
    far = jnp.sum(far, axis=-1, keepdims=True) + middle
    far, middle = far[:64] + far[64:], middle[:64] + middle[64:]

    for c in range(2 * CHUNKS):
        fetch(c).wait()
    sums = []
    for part in range(2):
        total = None
        for c in range(part * CHUNKS, (part + 1) * CHUNKS):
            left = left_ref[:, pl.ds(c * depth, depth)]
            term = jnp.dot(left, table_ref[c], preferred_element_type=f32)
            total = term if total is None else total + term
        near, away = total[:64] + total[64:128], total[128:192] + total[192:]
        sums.append((near[:, :256] + away[:, :256], near[:, 256:] - away[:, 256:]))
    (even_cosine, odd_cosine), (even_sine, odd_sine) = sums
    even_cosine, odd_cosine = even_cosine + middle, odd_cosine - middle
    lane = lax.broadcasted_iota(jnp.int32, (64, LANES), 1)
    for q in range(2):
        run = slice(q * LANES, (q + 1) * LANES)
        c, s = even_cosine[:, run], even_sine[:, run]
        minus, plus = c + s, c - s
        if q == 0:
            minus, plus = jnp.where(lane == 0, far + s, minus), jnp.where(lane == 0, c, plus)
        c, s = odd_cosine[:, run], odd_sine[:, run]
        for place, lags in ((q, minus), (q + 2, c + s), (q + 4, plus), (q + 6, c - s)):
            turn_ref[pl.ds(place, 64, stride=8), :] = lags * (2.0 * NF**-0.5)
    turned = turn_ref[...].reshape(2, 2, 16, 8, LANES)
    keep_ref[...] = turned[:, 0].astype(bf16)
    send_ref[...] = turned[:, 1].astype(bf16)


def correlate(pairs, spectra):
    half = jax.ShapeDtypeStruct((2, 16, 8, LANES), jnp.bfloat16)
    vmem = pl.BlockSpec(memory_space=pltpu.VMEM)
    tables = pltpu.with_memory_space_constraint(jnp.asarray(lag_tables()), pltpu.HBM)
    return pl.pallas_call(
        lag_kernel,
        out_shape=(half, half),
        in_specs=[vmem, vmem, pl.BlockSpec(memory_space=pltpu.HBM)],
        out_specs=(vmem, vmem),
        scratch_shapes=[
            pltpu.VMEM((128 * TURN, LANES), jnp.float32),
            pltpu.VMEM((256, NF // 2), jnp.bfloat16),
            pltpu.VMEM(tables.shape, jnp.bfloat16),
            pltpu.VMEM((64 * 8, LANES), jnp.float32),
            pltpu.SemaphoreType.DMA((2 * CHUNKS,)),
        ],
        compiler_params=pltpu.CompilerParams(vmem_limit_bytes=24 * 2**20),
        name="correlate",
    )(pairs, spectra, tables)


def stack_kernel(lags_ref, out_ref, turn_ref):
    total = lags_ref[0].astype(jnp.float32)
    for t in range(1, 4):
        total = total + lags_ref[t].astype(jnp.float32)
    turn_ref[...] = total.reshape(16 * 8, LANES)
    runs = [turn_ref[pl.ds(q, 16, stride=8), :] for q in range(8)]
    lane = lax.broadcasted_iota(jnp.int32, (16, LANES), 1)

    def pick(run, index):
        return jnp.take_along_axis(run, index, axis=1, mode="promise_in_bounds")

    for q in range(4):
        index = 64 * (q % 2) + lane // 2
        even, odd = pick(runs[4 + q // 2], index), pick(runs[6 + q // 2], index)
        out_ref[0, :, pl.ds((4 + q) * LANES, LANES)] = jnp.where(lane % 2 == 0, even, odd)
    for q in range(4):
        b, after = 3 - q, (4 - q) % 4
        even = pick(runs[b // 2], 64 * (b % 2) + (64 - lane // 2) % 64)
        first = pick(runs[after // 2], jnp.full_like(lane, 64 * (after % 2)))
        odd = pick(runs[2 + b // 2], 64 * (b % 2) + 63 - lane // 2)
        even = jnp.where(lane == 0, first, even)
        out_ref[0, :, pl.ds(q * LANES, LANES)] = jnp.where(lane % 2 == 0, even, odd)


def stack(lags):
    vmem = pl.BlockSpec(memory_space=pltpu.VMEM)
    return pl.pallas_call(
        stack_kernel,
        out_shape=jax.ShapeDtypeStruct((1, 16, LAGS), jnp.float32),
        in_specs=[vmem],
        out_specs=vmem,
        scratch_shapes=[pltpu.VMEM((16 * 8, LANES), jnp.float32)],
        name="stack",
    )(lags)


def body(raw, pair_blocks):
    core = lax.axis_index("blk") % 2
    near = [[32 * (2 * t + h) + d for h in range(2) for d in range(32)] for t in range(4)]
    far = [
        [32 * (2 * t + h) + 2 * chip + c for t in range(4) for chip in range(16)]
        for h in range(2)
        for c in range(2)
    ]
    spectra = whiten(raw).reshape(64, 2 * 2 * SLOTS, LANES)
    spectra = lax.all_to_all(spectra, AXES, 0, 0, axis_index_groups=near, tiled=True)
    spectra = spectra.reshape(64, 2, 2 * SLOTS, LANES)
    order = pair_blocks.reshape(16, 2, 2)
    order = jnp.where(core == 0, order, order[:, ::-1]).transpose(1, 0, 2).reshape(32, 2)
    order = jnp.pad(order, ((0, 0), (0, LANES - 2)))
    keep, send = correlate(order, spectra)
    got = lax.ppermute(send, "blk", [(i, i ^ 1) for i in range(32)])
    lags = jnp.where(core == 0, jnp.stack([keep, got]), jnp.stack([got, keep]))
    lags = lax.all_to_all(lags.reshape(64, 8, LANES), AXES, 0, 0, axis_index_groups=far, tiled=True)
    return stack(pltpu.with_memory_space_constraint(lags.reshape(4, 16, 8, LANES), pltpu.VMEM))


def solution(mesh):
    in_specs = (P("section", "blk", None), P())
    out_specs = P("blk", "section", None)
    return jax.shard_map(body, mesh=mesh, in_specs=in_specs, out_specs=out_specs, check_vma=False)
```

time: 77.7 us -> 75.8 us (0.976)
  Pallas kernels: 13.7 us -> 11.9 us
    pallas_call x1, Pallas kernels: 1.63 us -> 0.8 us  [stack(): pl.pallas_call(stack_kernel, out_shape=jax.ShapeDtypeStruct((1, 16, LAGS)...]
where the time goes in v3:
time: 75.8 us; the launch traced here: 74.9 us
  waiting for transfers between devices  28.6 us (38%)
  blocking collectives  24.3 us (32%)
  Pallas kernels  11.9 us (16%)
  starting transfers between devices  9.59 us (13%)
    all_to_all x1, waiting for transfers between devices, body(): lax.all_to_all(spectra, AXES, 0, 0, axis_index_groups=near, tiled=True)  27.4 us
    all_to_all x1, blocking collectives, body(): lax.all_to_all(lags.reshape(64, 8, LANES), AXES, 0, 0, axis_index_groups=...  24.3 us
    all_to_all x1, starting transfers between devices, body(): lax.all_to_all(spectra, AXES, 0, 0, axis_index_groups=near, tiled=True)  9.38 us
    pallas_call x1, Pallas kernels, whiten(): pl.pallas_call(whiten_kernel, out_shape=jax.ShapeDtypeStruct((2, 16, 2, 2...  7.25 us
    pallas_call x1, Pallas kernels, correlate(): pl.pallas_call(lag_kernel, out_shape=(half, half), in_specs=[vmem, vmem,...  3.89 us
  transfers between devices with their start and end apart: 2, of which 2 were waited for; matrix products, arithmetic and copies ran while one was open for 0% of the time, Pallas kernels for 0%

profile of v3, /device:TPU:2, one launch (start us, length us, event | category | flops | bytes accessed | tf_op | source)
XLA Modules:
  0.0 74.9 jit_solution(17276127054516560122)
XLA Ops:
  0.0 7.2 %whiten.1 = bf16[2,16,2,2,64,128]{5,4,3,2,1,0:T(8,128)(2,1)} custom-call(bf16[1,128,8192]{2,1,0:T(8,128)(2,1)} %raw_hbm.1, f32[2,32,128]{2,1,0:T(8,128)} %constant.24.clone.twist_hbm, f32[256,256]{1,0:T(8,128)} %constant.25.clone.last_hbm), custom_call_target="tpu_custom_call" | custom-call | tf_op jit(solution)/shard_map/whiten/pallas_call | solution.py:242
  7.3 0.0 copy-start
  7.3 9.4 %all-to-all-start = ((bf16[64,128,128]{2,1,0:T(8,128)(2,1)}), bf16[64,128,128]{2,1,0:T(8,128)(2,1)S(1)}, u32[]{:S(2)}, u32[]{:S(2)}) async-start(bf16[64,128,128]{2,1,0:T(8,128)(2,1)} %bitcast.14), calls=%async_computation | async-start | bytes 4194304 | tf_op jit(solution)/shard_map/all_to_all | solution.py:412
  16.7 0.0 copy-done
  16.7 0.1 reshape.20
  16.8 0.1 rev.3
  16.8 0.2 copy.10
  17.1 27.4 %all-to-all-done = bf16[64,128,128]{2,1,0:T(8,128)(2,1)S(1)} async-done(((bf16[64,128,128]{2,1,0:T(8,128)(2,1)}), bf16[64,128,128]{2,1,0:T(8,128)(2,1)S(1)}, u32[]{:S(2)}, u32[]{:S(2)}) %all-to-all-start) | async-done | bytes 2097184 | tf_op jit(solution)/shard_map/all_to_all | solution.py:412
  44.5 3.9 %correlate.1 = (bf16[2,16,8,128]{3,2,1,0:T(8,128)(2,1)S(1)}, bf16[2,16,8,128]{3,2,1,0:T(8,128)(2,1)S(1)}) custom-call(s32[32,128]{1,0:T(8,128)S(1)} %pad.4.pairs_ref, bf16[64,2,64,128]{3,2,1,0:T(8,128)(2,1)S(1)} %bitcast.11, bf16[8,512,512]{2,1,0:T(8,128)(2,1)} %constant.26.clone.table_hbm), custom_call_target="tpu_custom_call" | custom-call | tf_op jit(solution)/shard_map/correlate/pallas_call | solution.py:350
  48.4 0.2 collective-permute-start
  48.6 1.1 %collective-permute-done = bf16[2,16,8,128]{3,2,1,0:T(8,128)(2,1)S(1)} collective-permute-done((bf16[2,16,8,128]{3,2,1,0:T(8,128)(2,1)S(1)}, bf16[2,16,8,128]{3,2,1,0:T(8,128)(2,1)S(1)}, u32[]{:S(2)}, u32[]{:S(2)}) %collective-permute-start) | collective-permute-done | bytes 65568 | tf_op jit(solution)/shard_map/ppermute | solution.py:418
  49.8 24.3 %all_to_all.10 = bf16[64,8,128]{2,1,0:T(8,128)(2,1)S(1)} all-to-all(bf16[64,8,128]{2,1,0:T(8,128)(2,1)S(1)} %bitcast.15), channel_id=1, replica_groups={{0,2,4,6,8,10,12,14,16,18,20,22,24,26,28,30,64,66,68,70,72,74,76,78,80,..., dimensions={0} | all-to-all | bytes 262144 | tf_op jit(solution)/shard_map/all_to_all | solution.py:420
  74.1 0.8 %stack.19 = f32[1,16,1024]{2,1,0:T(8,128)} custom-call(bf16[4,16,8,128]{3,2,1,0:T(8,128)(2,1)S(1)} %bitcast.12), custom_call_target="tpu_custom_call" | custom-call | tf_op jit(solution)/shard_map/stack/pallas_call | solution.py:393
  (3 shorter events, 0.0 us)
Async XLA Ops:
  7.3 9.4 %copy-start = (s32[32,2]{0,1:T(2,128)S(1)}, s32[32,2]{0,1:T(2,128)}, u32[]{:S(2)}) copy-start(s32[32,2]{0,1:T(2,128)} %param.6) | copy-start | bytes 772
  7.3 37.2 %all-to-all-start = ((bf16[64,128,128]{2,1,0:T(8,128)(2,1)}), bf16[64,128,128]{2,1,0:T(8,128)(2,1)S(1)}, u32[]{:S(2)}, u32[]{:S(2)}) async-start(bf16[64,128,128]{2,1,0:T(8,128)(2,1)} %bitcast.14), calls=%async_computation | async-start | bytes 4194304 | tf_op jit(solution)/shard_map/all_to_all | solution.py:412
  48.4 1.3 %collective-permute-start = (bf16[2,16,8,128]{3,2,1,0:T(8,128)(2,1)S(1)}, bf16[2,16,8,128]{3,2,1,0:T(8,128)(2,1)S(1)}, u32[]{:S(2)}, u32[]{:S(2)}) collective-permute-start(bf16[2,16,8,128]{3,2,1,0:T(8,128)(2,1)S(1)} %get-tuple-element.8), channel_id=1, source_target_pairs={{0,1},{1,0},{2,3},{3,2},{4,5},{5,4},{6,7},{7,6},{8,9},{9,8},{10,11... | collective-permute-start | bytes 196616 | tf_op jit(solution)/shard_map/ppermute | solution.py:418

commit v4 on v3

--- a/solution.py
+++ b/solution.py
@@ -12,8 +12,9 @@
 NF = 8192
 LAGS = 1024
 LANES = 128
-ROWS = 32
-STEPS = 4
+ROWS = 64
+STEPS = 2
+PART = 32
 SLOTS = 32
 TURN = 72
 CHUNKS = 4
@@ -45,7 +46,14 @@
     angle = 2.0 * np.pi * (index[:, None] * index[None, :] % LANES) / LANES
     cosine, sine = np.cos(angle), np.sin(angle)
     full = np.block([[cosine, -sine], [sine, cosine]])
-    return full.astype(np.float32)
+    high = full.astype(ml_dtypes.bfloat16)
+    low = (full - high.astype(np.float64)).astype(ml_dtypes.bfloat16)
+    return np.concatenate([high, high, low])
+
+
+def folded_bins():
+    bins = bin_numbers()
+    return np.concatenate([bins[:16, :64], bins[16:, :64]], axis=1)
 
 
 def folded_bins():
@@ -113,9 +121,22 @@
 
 def outer_transform(raw_ref, twist_ref, turned_ref, part_ref):
     f32 = jnp.float32
-
+    for first in range(0, ROWS, 32):
+        rows = pl.ds(first, 32)
+        for b in range(8):
+            x = [raw_ref[rows, pl.ds((8 * a + b) * LANES, LANES)].astype(f32) for a in range(8)]
+            y = real8(x)
+            for q in range(5):
+                part_ref[0, q, b, rows] = y[q][0]
+                if y[q][1] is not None:
+                    part_ref[1, q, b, rows] = y[q][1]
+    for first in range(0, ROWS, 8):
+        second_transform(first, 8, twist_ref, turned_ref, part_ref)
+
+
+def second_transform(first, count, twist_ref, turned_ref, part_ref):
     def put(slot, re, im):
-        rows = pl.ds(slot * ROWS, ROWS)
+        rows = pl.ds(slot * ROWS + first, count)
         turned_ref[rows, pl.ds(0, LANES)] = re
         turned_ref[rows, pl.ds(LANES, LANES)] = im
 
@@ -126,14 +147,10 @@
         else:
             put(slot, re * cosine + im * sine, im * cosine - re * sine)
 
-    for b in range(8):
-        x = [raw_ref[:, pl.ds((8 * a + b) * LANES, LANES)].astype(f32) for a in range(8)]
-        y = real8(x)
-        for q in range(5):
-            part_ref[0, q, b] = y[q][0]
-            if y[q][1] is not None:
-                part_ref[1, q, b] = y[q][1]
-    whole = real8([part_ref[0, 0, b] for b in range(8)])
+    def part(side, q, b):
+        return part_ref[side, q, b, pl.ds(first, count)]
+
+    whole = real8([part(0, 0, b) for b in range(8)])
     zero = whole[0][0]
     put(0, zero - jnp.mean(zero, axis=-1, keepdims=True), jnp.zeros_like(zero))
     turn(1, whole[4][0], None)
@@ -144,12 +161,12 @@
         re, im = [], []
         for b in range(8):
             cosine, sine = math.cos(2 * math.pi * b * q / 64), math.sin(2 * math.pi * b * q / 64)
-            yr = part_ref[0, q, b]
+            yr = part(0, q, b)
             if q == 4:
                 re.append(yr * cosine if b else yr)
                 im.append(yr * -sine if b else jnp.zeros_like(yr))
             else:
-                yi = part_ref[1, q, b]
+                yi = part(1, q, b)
                 re.append(yr * cosine + yi * sine if b else yr)
                 im.append(yi * cosine - yr * sine if b else yi)
         z = complex8(re, im)
@@ -157,23 +174,27 @@
             turn(slot, *z[r])
             slot += 1
 
+
 def inner_transform(last_ref, turned_ref, spec_ref):
+    left = turned_ref[...]
+    high = left.astype(jnp.bfloat16)
+    low = (left - high.astype(jnp.float32)).astype(jnp.bfloat16)
     spec_ref[...] = jnp.dot(
-        turned_ref[...], last_ref[...], preferred_element_type=jnp.float32, precision=lax.Precision.HIGH
+        jnp.concatenate([high, low, high], axis=1), last_ref[...], preferred_element_type=jnp.float32
     )
 
 
-def level_rows(spec_ref, out_ref, turn_ref):
+def level_rows(spec_ref, out_ref, turn_ref, first):
     bf16 = jnp.bfloat16
-    lane = lax.broadcasted_iota(jnp.int32, (ROWS, LANES), 1)
+    lane = lax.broadcasted_iota(jnp.int32, (PART, LANES), 1)
 
     for lanes in (pl.ds(0, LANES), pl.ds(LANES, LANES)):
-        whole, moved = spec_ref[pl.ds(0, ROWS), lanes], spec_ref[pl.ds(ROWS, ROWS), lanes]
+        whole, moved = spec_ref[pl.ds(first, PART), lanes], spec_ref[pl.ds(ROWS + first, PART), lanes]
         whole = jnp.where(lane == 0, pltpu.roll(whole, 96, 1), whole)
-        spec_ref[pl.ds(ROWS, ROWS), lanes] = jnp.where(lane % 64 < 32, whole, moved)
+        spec_ref[pl.ds(ROWS + first, PART), lanes] = jnp.where(lane % 64 < 32, whole, moved)
 
     def get(slot):
-        rows = pl.ds((slot + 1) * ROWS, ROWS)
+        rows = pl.ds((slot + 1) * ROWS + first, PART)
         return spec_ref[rows, pl.ds(0, LANES)], spec_ref[rows, pl.ds(LANES, LANES)]
 
     total = None
@@ -184,14 +205,14 @@
             power = jnp.where(lane == 64, power * 0.5, power)
         total = power if total is None else total + power
     level = jnp.sum(total, axis=-1, keepdims=True) * (2.0 / NF)
-    floor = jnp.broadcast_to(0.1 * level + 1e-06, (ROWS, LANES))
+    floor = jnp.broadcast_to(0.1 * level + 1e-06, (PART, LANES))
     for slot in range(SLOTS):
         re, im = get(slot)
         scale = lax.rsqrt(re * re + im * im + floor)
-        turn_ref[pl.ds(slot, ROWS, stride=TURN), :] = re * scale
-        turn_ref[pl.ds(slot + SLOTS, ROWS, stride=TURN), :] = im * scale
-    for r in range(ROWS):
-        out_ref[r // 16, r % 16] = turn_ref[pl.ds(r * TURN, 2 * SLOTS), :].astype(bf16)
+        turn_ref[pl.ds(first * TURN + slot, PART, stride=TURN), :] = re * scale
+        turn_ref[pl.ds(first * TURN + slot + SLOTS, PART, stride=TURN), :] = im * scale
+    for r in range(PART):
+        out_ref[r // 16, r % 16] = turn_ref[pl.ds((first + r) * TURN, 2 * SLOTS), :].astype(bf16)
 
 
 def whiten_kernel(
@@ -200,8 +221,8 @@
     def fetch(g):
         return pltpu.make_async_copy(raw_hbm.at[0, pl.ds(g * ROWS, ROWS)], raw_ref.at[g], in_sem.at[g])
 
-    def leave(g):
-        return pltpu.make_async_copy(out_ref.at[g], out_hbm.at[:, :, g // 2, g % 2], out_sem.at[g])
+    def leave(g, j):
+        return pltpu.make_async_copy(out_ref.at[g, j], out_hbm.at[:, :, g, j], out_sem.at[g, j])
 
     twist = pltpu.make_async_copy(twist_hbm, twist_ref, table_sem.at[0])
     last = pltpu.make_async_copy(last_hbm, last_ref, table_sem.at[1])
@@ -220,21 +241,20 @@
     outer(0)
     last.wait()
 
-    def step(g, carry):
-        fetch(g + 1).wait()
-        inner_transform(last_ref, turned, spec)
-        outer(g + 1)
-        level_rows(spec, out_ref.at[g], turn)
-
-        leave(g).start()
-        return carry
-
-    lax.fori_loop(0, STEPS - 1, step, 0)
+    def level(g):
+        for j in range(2):
+            level_rows(spec, out_ref.at[g, j], turn, j * PART)
+            leave(g, j).start()
+
+    fetch(1).wait()
     inner_transform(last_ref, turned, spec)
-    level_rows(spec, out_ref.at[STEPS - 1], turn)
-    leave(STEPS - 1).start()
+    outer(1)
+    level(0)
+    inner_transform(last_ref, turned, spec)
+    level(1)
     for g in range(STEPS):
-        leave(g).wait()
+        for j in range(2):
+            leave(g, j).wait()
 
 
 def whiten(raw):
@@ -247,17 +267,15 @@
         scratch_shapes=[
             pltpu.VMEM((STEPS, ROWS, NF), jnp.bfloat16),
             pltpu.VMEM((2, SLOTS, LANES), jnp.float32),
-            pltpu.VMEM((2 * LANES, 2 * LANES), jnp.float32),
-            pltpu.VMEM((STEPS, 2, 16, 2 * SLOTS, LANES), jnp.bfloat16),
+            pltpu.VMEM((6 * LANES, 2 * LANES), jnp.bfloat16),
+            pltpu.VMEM((STEPS, 2, 2, 16, 2 * SLOTS, LANES), jnp.bfloat16),
             pltpu.SemaphoreType.DMA((STEPS,)),
             pltpu.SemaphoreType.DMA((2,)),
-            pltpu.SemaphoreType.DMA((STEPS,)),
-        ]
-        + [
+            pltpu.SemaphoreType.DMA((STEPS, 2)),
             pltpu.VMEM((2, 5, 8, ROWS, LANES), jnp.float32),
             pltpu.VMEM(((SLOTS + 1) * ROWS, 2 * LANES), jnp.float32),
             pltpu.VMEM(((SLOTS + 1) * ROWS, 2 * LANES), jnp.float32),
-            pltpu.VMEM((ROWS * TURN, LANES), jnp.float32),
+            pltpu.VMEM((ROWS * TURN + TURN, LANES), jnp.float32),
         ],
         compiler_params=pltpu.CompilerParams(vmem_limit_bytes=60 * 2**20),
         name="whiten",
@@ -338,7 +356,7 @@
         c, s = odd_cosine[:, run], odd_sine[:, run]
         for place, lags in ((q, minus), (q + 2, c + s), (q + 4, plus), (q + 6, c - s)):
             turn_ref[pl.ds(place, 64, stride=8), :] = lags * (2.0 * NF**-0.5)
-    turned = turn_ref[...].reshape(2, 2, 16, 8, LANES)
+    turned = turn_ref[pl.ds(0, 64 * 8), :].reshape(2, 2, 16, 8, LANES)
     keep_ref[...] = turned[:, 0].astype(bf16)
     send_ref[...] = turned[:, 1].astype(bf16)
 
@@ -353,10 +371,10 @@
         in_specs=[vmem, vmem, pl.BlockSpec(memory_space=pltpu.HBM)],
         out_specs=(vmem, vmem),
         scratch_shapes=[
-            pltpu.VMEM((128 * TURN, LANES), jnp.float32),
+            pltpu.VMEM((128 * TURN + TURN, LANES), jnp.float32),
             pltpu.VMEM((256, NF // 2), jnp.bfloat16),
             pltpu.VMEM(tables.shape, jnp.bfloat16),
-            pltpu.VMEM((64 * 8, LANES), jnp.float32),
+            pltpu.VMEM((64 * 8 + 8, LANES), jnp.float32),
             pltpu.SemaphoreType.DMA((2 * CHUNKS,)),
         ],
         compiler_params=pltpu.CompilerParams(vmem_limit_bytes=24 * 2**20),
@@ -368,7 +386,7 @@
     total = lags_ref[0].astype(jnp.float32)
     for t in range(1, 4):
         total = total + lags_ref[t].astype(jnp.float32)
-    turn_ref[...] = total.reshape(16 * 8, LANES)
+    turn_ref[pl.ds(0, 16 * 8), :] = total.reshape(16 * 8, LANES)
     runs = [turn_ref[pl.ds(q, 16, stride=8), :] for q in range(8)]
     lane = lax.broadcasted_iota(jnp.int32, (16, LANES), 1)
 
@@ -395,7 +413,7 @@
         out_shape=jax.ShapeDtypeStruct((1, 16, LAGS), jnp.float32),
         in_specs=[vmem],
         out_specs=vmem,
-        scratch_shapes=[pltpu.VMEM((16 * 8, LANES), jnp.float32)],
+        scratch_shapes=[pltpu.VMEM((16 * 8 + 8, LANES), jnp.float32)],
         name="stack",
     )(lags)
 

time: 75.8 us -> 75.4 us (level)
  transfers between devices with their start and end apart: 2 -> 2, of which waited for: 2 -> 2; matrix products, arithmetic and copies ran while one was open for 0% -> 1% of each run, Pallas kernels for 0% -> 0%
where the time goes in v4:
time: 75.4 us; the launch traced here: 74.5 us
  waiting for transfers between devices  28.6 us (38%)
  blocking collectives  24.3 us (32%)
  Pallas kernels  11.5 us (15%)
  starting transfers between devices  9.59 us (13%)
    all_to_all x1, waiting for transfers between devices, body(): lax.all_to_all(spectra, AXES, 0, 0, axis_index_groups=near, tiled=True)  27.4 us
    all_to_all x1, blocking collectives, body(): lax.all_to_all(lags.reshape(64, 8, LANES), AXES, 0, 0, axis_index_groups=...  24.3 us
    all_to_all x1, starting transfers between devices, body(): lax.all_to_all(spectra, AXES, 0, 0, axis_index_groups=near, tiled=True)  9.39 us
    pallas_call x1, Pallas kernels, whiten(): pl.pallas_call(whiten_kernel, out_shape=jax.ShapeDtypeStruct((2, 16, 2, 2...  6.83 us
    pallas_call x1, Pallas kernels, correlate(): pl.pallas_call(lag_kernel, out_shape=(half, half), in_specs=[vmem, vmem,...  3.89 us
  transfers between devices with their start and end apart: 2, of which 2 were waited for; matrix products, arithmetic and copies ran while one was open for 1% of the time, Pallas kernels for 0%

profile of v4, /device:TPU:2, one launch (start us, length us, event | category | flops | bytes accessed | tf_op | source)
XLA Modules:
  0.0 74.5 jit_solution(16874074860783428094)
XLA Ops:
  0.0 6.8 %whiten.1 = bf16[2,16,2,2,64,128]{5,4,3,2,1,0:T(8,128)(2,1)} custom-call(bf16[1,128,8192]{2,1,0:T(8,128)(2,1)} %raw_hbm.1, f32[2,32,128]{2,1,0:T(8,128)} %constant.24.clone.twist_hbm, bf16[768,256]{1,0:T(8,128)(2,1)} %constant.25.clone.last_hbm), custom_call_target="tpu_custom_call" | custom-call | tf_op jit(solution)/shard_map/whiten/pallas_call | solution.py:262
  6.8 0.0 copy-start
  6.9 9.4 %all-to-all-start = ((bf16[64,128,128]{2,1,0:T(8,128)(2,1)}), bf16[64,128,128]{2,1,0:T(8,128)(2,1)S(1)}, u32[]{:S(2)}, u32[]{:S(2)}) async-start(bf16[64,128,128]{2,1,0:T(8,128)(2,1)} %bitcast.14), calls=%async_computation | async-start | bytes 4194304 | tf_op jit(solution)/shard_map/all_to_all | solution.py:430
  16.3 0.0 copy-done
  16.3 0.1 reshape.20
  16.4 0.1 rev.3
  16.4 0.2 copy.10
  16.6 27.4 %all-to-all-done = bf16[64,128,128]{2,1,0:T(8,128)(2,1)S(1)} async-done(((bf16[64,128,128]{2,1,0:T(8,128)(2,1)}), bf16[64,128,128]{2,1,0:T(8,128)(2,1)S(1)}, u32[]{:S(2)}, u32[]{:S(2)}) %all-to-all-start) | async-done | bytes 2097184 | tf_op jit(solution)/shard_map/all_to_all | solution.py:430
  44.1 3.9 %correlate.1 = (bf16[2,16,8,128]{3,2,1,0:T(8,128)(2,1)S(1)}, bf16[2,16,8,128]{3,2,1,0:T(8,128)(2,1)S(1)}) custom-call(s32[32,128]{1,0:T(8,128)S(1)} %pad.4.pairs_ref, bf16[64,2,64,128]{3,2,1,0:T(8,128)(2,1)S(1)} %bitcast.11, bf16[8,512,512]{2,1,0:T(8,128)(2,1)} %constant.26.clone.table_hbm), custom_call_target="tpu_custom_call" | custom-call | tf_op jit(solution)/shard_map/correlate/pallas_call | solution.py:368
  48.0 0.2 collective-permute-start
  48.2 1.1 %collective-permute-done = bf16[2,16,8,128]{3,2,1,0:T(8,128)(2,1)S(1)} collective-permute-done((bf16[2,16,8,128]{3,2,1,0:T(8,128)(2,1)S(1)}, bf16[2,16,8,128]{3,2,1,0:T(8,128)(2,1)S(1)}, u32[]{:S(2)}, u32[]{:S(2)}) %collective-permute-start) | collective-permute-done | bytes 65568 | tf_op jit(solution)/shard_map/ppermute | solution.py:436
  49.3 24.3 %all_to_all.10 = bf16[64,8,128]{2,1,0:T(8,128)(2,1)S(1)} all-to-all(bf16[64,8,128]{2,1,0:T(8,128)(2,1)S(1)} %bitcast.15), channel_id=1, replica_groups={{0,2,4,6,8,10,12,14,16,18,20,22,24,26,28,30,64,66,68,70,72,74,76,78,80,..., dimensions={0} | all-to-all | bytes 262144 | tf_op jit(solution)/shard_map/all_to_all | solution.py:438
  73.7 0.8 %stack.19 = f32[1,16,1024]{2,1,0:T(8,128)} custom-call(bf16[4,16,8,128]{3,2,1,0:T(8,128)(2,1)S(1)} %bitcast.12), custom_call_target="tpu_custom_call" | custom-call | tf_op jit(solution)/shard_map/stack/pallas_call | solution.py:411
  (3 shorter events, 0.0 us)
Async XLA Ops:
  6.8 9.4 %copy-start = (s32[32,2]{0,1:T(2,128)S(1)}, s32[32,2]{0,1:T(2,128)}, u32[]{:S(2)}) copy-start(s32[32,2]{0,1:T(2,128)} %param.6) | copy-start | bytes 772
  6.9 37.2 %all-to-all-start = ((bf16[64,128,128]{2,1,0:T(8,128)(2,1)}), bf16[64,128,128]{2,1,0:T(8,128)(2,1)S(1)}, u32[]{:S(2)}, u32[]{:S(2)}) async-start(bf16[64,128,128]{2,1,0:T(8,128)(2,1)} %bitcast.14), calls=%async_computation | async-start | bytes 4194304 | tf_op jit(solution)/shard_map/all_to_all | solution.py:430
  48.0 1.3 %collective-permute-start = (bf16[2,16,8,128]{3,2,1,0:T(8,128)(2,1)S(1)}, bf16[2,16,8,128]{3,2,1,0:T(8,128)(2,1)S(1)}, u32[]{:S(2)}, u32[]{:S(2)}) collective-permute-start(bf16[2,16,8,128]{3,2,1,0:T(8,128)(2,1)S(1)} %get-tuple-element.8), channel_id=1, source_target_pairs={{0,1},{1,0},{2,3},{3,2},{4,5},{5,4},{6,7},{7,6},{8,9},{9,8},{10,11... | collective-permute-start | bytes 196616 | tf_op jit(solution)/shard_map/ppermute | solution.py:436

commit v5 on v4

--- a/solution.py
+++ b/solution.py
@@ -15,6 +15,7 @@
 ROWS = 64
 STEPS = 2
 PART = 32
+PIECES = 2
 SLOTS = 32
 TURN = 72
 CHUNKS = 4
@@ -218,26 +219,30 @@
 def whiten_kernel(
     raw_hbm, twist_hbm, last_hbm, out_hbm, raw_ref, twist_ref, last_ref, out_ref, in_sem, table_sem, out_sem, *work
 ):
-    def fetch(g):
-        return pltpu.make_async_copy(raw_hbm.at[0, pl.ds(g * ROWS, ROWS)], raw_ref.at[g], in_sem.at[g])
+    def fetch(g, part):
+        rows = pl.ds(part * 32, 32)
+        source = raw_hbm.at[0, pl.ds(g * ROWS + part * 32, 32)]
+        return pltpu.make_async_copy(source, raw_ref.at[g, rows], in_sem.at[g, part])
 
     def leave(g, j):
         return pltpu.make_async_copy(out_ref.at[g, j], out_hbm.at[:, :, g, j], out_sem.at[g, j])
 
     twist = pltpu.make_async_copy(twist_hbm, twist_ref, table_sem.at[0])
     last = pltpu.make_async_copy(last_hbm, last_ref, table_sem.at[1])
-    fetch(0).start()
+    for p in range(PIECES):
+        fetch(0, p).start()
     twist.start()
     last.start()
-    for g in range(1, STEPS):
-        fetch(g).start()
+    for p in range(PIECES):
+        fetch(1, p).start()
     part, turned, spec, turn = work
 
     def outer(g):
         outer_transform(raw_ref.at[g], twist_ref, turned, part)
 
     twist.wait()
-    fetch(0).wait()
+    for p in range(PIECES):
+        fetch(0, p).wait()
     outer(0)
     last.wait()
 
@@ -246,7 +251,8 @@
             level_rows(spec, out_ref.at[g, j], turn, j * PART)
             leave(g, j).start()
 
-    fetch(1).wait()
+    for p in range(PIECES):
+        fetch(1, p).wait()
     inner_transform(last_ref, turned, spec)
     outer(1)
     level(0)
@@ -269,7 +275,7 @@
             pltpu.VMEM((2, SLOTS, LANES), jnp.float32),
             pltpu.VMEM((6 * LANES, 2 * LANES), jnp.bfloat16),
             pltpu.VMEM((STEPS, 2, 2, 16, 2 * SLOTS, LANES), jnp.bfloat16),
-            pltpu.SemaphoreType.DMA((STEPS,)),
+            pltpu.SemaphoreType.DMA((STEPS, PIECES)),
             pltpu.SemaphoreType.DMA((2,)),
             pltpu.SemaphoreType.DMA((STEPS, 2)),
             pltpu.VMEM((2, 5, 8, ROWS, LANES), jnp.float32),

time: 75.4 us -> 75.4 us (level)
  no operation moved by 1% of the time
where the time goes in v5:
time: 75.4 us; the launch traced here: 74.5 us
  waiting for transfers between devices  28.6 us (38%)
  blocking collectives  24.3 us (32%)
  Pallas kernels  11.5 us (15%)
  starting transfers between devices  9.59 us (13%)
    all_to_all x1, waiting for transfers between devices, body(): lax.all_to_all(spectra, AXES, 0, 0, axis_index_groups=near, tiled=True)  27.4 us
    all_to_all x1, blocking collectives, body(): lax.all_to_all(lags.reshape(64, 8, LANES), AXES, 0, 0, axis_index_groups=...  24.3 us
    all_to_all x1, starting transfers between devices, body(): lax.all_to_all(spectra, AXES, 0, 0, axis_index_groups=near, tiled=True)  9.39 us
    pallas_call x1, Pallas kernels, whiten(): pl.pallas_call(whiten_kernel, out_shape=jax.ShapeDtypeStruct((2, 16, 2, 2...  6.82 us
    pallas_call x1, Pallas kernels, correlate(): pl.pallas_call(lag_kernel, out_shape=(half, half), in_specs=[vmem, vmem,...  3.89 us
  transfers between devices with their start and end apart: 2, of which 2 were waited for; matrix products, arithmetic and copies ran while one was open for 1% of the time, Pallas kernels for 0%

profile of v5, /device:TPU:2, one launch (start us, length us, event | category | flops | bytes accessed | tf_op | source)
XLA Modules:
  0.0 74.5 jit_solution(4070847708838408926)
XLA Ops:
  0.0 6.8 %whiten.1 = bf16[2,16,2,2,64,128]{5,4,3,2,1,0:T(8,128)(2,1)} custom-call(bf16[1,128,8192]{2,1,0:T(8,128)(2,1)} %raw_hbm.1, f32[2,32,128]{2,1,0:T(8,128)} %constant.24.clone.twist_hbm, bf16[768,256]{1,0:T(8,128)(2,1)} %constant.25.clone.last_hbm), custom_call_target="tpu_custom_call" | custom-call | tf_op jit(solution)/shard_map/whiten/pallas_call | solution.py:268
  6.8 0.0 copy-start
  6.8 9.4 %all-to-all-start = ((bf16[64,128,128]{2,1,0:T(8,128)(2,1)}), bf16[64,128,128]{2,1,0:T(8,128)(2,1)S(1)}, u32[]{:S(2)}, u32[]{:S(2)}) async-start(bf16[64,128,128]{2,1,0:T(8,128)(2,1)} %bitcast.14), calls=%async_computation | async-start | bytes 4194304 | tf_op jit(solution)/shard_map/all_to_all | solution.py:436
  16.3 0.0 copy-done
  16.3 0.1 reshape.20
  16.3 0.1 rev.3
  16.4 0.2 copy.10
  16.6 27.4 %all-to-all-done = bf16[64,128,128]{2,1,0:T(8,128)(2,1)S(1)} async-done(((bf16[64,128,128]{2,1,0:T(8,128)(2,1)}), bf16[64,128,128]{2,1,0:T(8,128)(2,1)S(1)}, u32[]{:S(2)}, u32[]{:S(2)}) %all-to-all-start) | async-done | bytes 2097184 | tf_op jit(solution)/shard_map/all_to_all | solution.py:436
  44.1 3.9 %correlate.1 = (bf16[2,16,8,128]{3,2,1,0:T(8,128)(2,1)S(1)}, bf16[2,16,8,128]{3,2,1,0:T(8,128)(2,1)S(1)}) custom-call(s32[32,128]{1,0:T(8,128)S(1)} %pad.4.pairs_ref, bf16[64,2,64,128]{3,2,1,0:T(8,128)(2,1)S(1)} %bitcast.11, bf16[8,512,512]{2,1,0:T(8,128)(2,1)} %constant.26.clone.table_hbm), custom_call_target="tpu_custom_call" | custom-call | tf_op jit(solution)/shard_map/correlate/pallas_call | solution.py:374
  48.0 0.2 collective-permute-start
  48.2 1.1 %collective-permute-done = bf16[2,16,8,128]{3,2,1,0:T(8,128)(2,1)S(1)} collective-permute-done((bf16[2,16,8,128]{3,2,1,0:T(8,128)(2,1)S(1)}, bf16[2,16,8,128]{3,2,1,0:T(8,128)(2,1)S(1)}, u32[]{:S(2)}, u32[]{:S(2)}) %collective-permute-start) | collective-permute-done | bytes 65568 | tf_op jit(solution)/shard_map/ppermute | solution.py:442
  49.3 24.3 %all_to_all.10 = bf16[64,8,128]{2,1,0:T(8,128)(2,1)S(1)} all-to-all(bf16[64,8,128]{2,1,0:T(8,128)(2,1)S(1)} %bitcast.15), channel_id=1, replica_groups={{0,2,4,6,8,10,12,14,16,18,20,22,24,26,28,30,64,66,68,70,72,74,76,78,80,..., dimensions={0} | all-to-all | bytes 262144 | tf_op jit(solution)/shard_map/all_to_all | solution.py:444
  73.7 0.8 %stack.19 = f32[1,16,1024]{2,1,0:T(8,128)} custom-call(bf16[4,16,8,128]{3,2,1,0:T(8,128)(2,1)S(1)} %bitcast.12), custom_call_target="tpu_custom_call" | custom-call | tf_op jit(solution)/shard_map/stack/pallas_call | solution.py:417
  (3 shorter events, 0.0 us)
Async XLA Ops:
  6.8 9.4 %copy-start = (s32[32,2]{0,1:T(2,128)S(1)}, s32[32,2]{0,1:T(2,128)}, u32[]{:S(2)}) copy-start(s32[32,2]{0,1:T(2,128)} %param.6) | copy-start | bytes 772
  6.8 37.2 %all-to-all-start = ((bf16[64,128,128]{2,1,0:T(8,128)(2,1)}), bf16[64,128,128]{2,1,0:T(8,128)(2,1)S(1)}, u32[]{:S(2)}, u32[]{:S(2)}) async-start(bf16[64,128,128]{2,1,0:T(8,128)(2,1)} %bitcast.14), calls=%async_computation | async-start | bytes 4194304 | tf_op jit(solution)/shard_map/all_to_all | solution.py:436
  48.0 1.3 %collective-permute-start = (bf16[2,16,8,128]{3,2,1,0:T(8,128)(2,1)S(1)}, bf16[2,16,8,128]{3,2,1,0:T(8,128)(2,1)S(1)}, u32[]{:S(2)}, u32[]{:S(2)}) collective-permute-start(bf16[2,16,8,128]{3,2,1,0:T(8,128)(2,1)S(1)} %get-tuple-element.8), channel_id=1, source_target_pairs={{0,1},{1,0},{2,3},{3,2},{4,5},{5,4},{6,7},{7,6},{8,9},{9,8},{10,11... | collective-permute-start | bytes 196616 | tf_op jit(solution)/shard_map/ppermute | solution.py:442
